TPU v7x, 32 devices: a whole 2x2x4 slice. The times are simulated.
32 devices in a mesh: row: 4 (over z), col: 4 (over y, x), dp: 2 (over core).
Axes of the slice: x: 2, y: 2, z: 4, core: 2. Of those that a mesh axis runs over, the one named last changes fastest.
Arguments:
- tokens: bfloat16 [2048, 8192], P(('col', 'dp'), 'row'), may hold values from -6 to 6
- out_grad: bfloat16 [2048, 8192], P(('col', 'dp'), 'row'), may hold values from -6 to 6
- weight_in: bfloat16 [8192, 16384], P('row', 'col'), may hold values from -0.0625 to 0.0625
- weight_out: bfloat16 [16384, 8192], P('col', 'row'), may hold values from -0.046875 to 0.046875
Outputs:
- mixed: bfloat16 [2048, 8192], P(('col', 'dp'), 'row')
- token_grad: bfloat16 [2048, 8192], P(('col', 'dp'), 'row')
- grad_in: float32 [8192, 16384], P('row', ('col', 'dp'))
- grad_out: float32 [16384, 8192], P(('col', 'dp'), 'row')
All inputs are finite; a program needn't handle non-finite values.
Results may differ from a plain program's by a relative error of at most 0.035.
Values may be sent and summed in bfloat16 or wider, within the bound.
A program may use at most 256 MiB of HBM per device.

v0:
```python
import math

import jax
import jax.numpy as jnp
from jax import lax
from jax.sharding import PartitionSpec as P


def gelu_parts(pre):
    cdf = 0.5 * (1.0 + jax.scipy.special.erf(pre * (1.0 / math.sqrt(2.0))))
    activated = pre * cdf
    slope = cdf + pre * jnp.exp(-0.5 * pre * pre) * (1.0 / math.sqrt(2.0 * math.pi))
    return (activated, slope)


def shards(tokens, out_grad, weight_in, weight_out):
    panel = lax.all_gather(tokens, "col", axis=0, tiled=True)
    count_all = panel.shape[0]
    factor = 1.0 / math.sqrt(count_all * lax.axis_size("dp"))
    pre = lax.psum_scatter(
        jnp.dot(panel, weight_in, preferred_element_type=jnp.float32).astype(jnp.bfloat16),
        "row",
        scatter_dimension=0,
        tiled=True,
    ).astype(jnp.float32)
    activated, slope = gelu_parts(pre)
    act = lax.all_gather(activated.astype(jnp.bfloat16), "row", axis=0, tiled=True)
    mixed = lax.psum_scatter(
        jnp.dot(act, weight_out, preferred_element_type=jnp.float32).astype(jnp.bfloat16),
        "col",
        scatter_dimension=0,
        tiled=True,
    )
    grad_panel = lax.all_gather(out_grad, "col", axis=0, tiled=True)
    out_local = lax.dot_general(
        act, grad_panel, (((0,), (0,)), ((), ())), preferred_element_type=jnp.float32
    )
    grad_out = (
        lax.psum_scatter(
            out_local.astype(jnp.bfloat16), "dp", scatter_dimension=0, tiled=True
        ).astype(jnp.float32)
        * factor
    )
    back = lax.psum_scatter(
        lax.dot_general(
            grad_panel, weight_out, (((1,), (1,)), ((), ())), preferred_element_type=jnp.float32
        ).astype(jnp.bfloat16),
        "row",
        scatter_dimension=0,
        tiled=True,
    ).astype(jnp.float32)
    dpre = lax.all_gather((back * slope).astype(jnp.bfloat16), "row", axis=0, tiled=True)
    token_grad = lax.psum_scatter(
        lax.dot_general(
            dpre, weight_in, (((1,), (1,)), ((), ())), preferred_element_type=jnp.float32
        ).astype(jnp.bfloat16),
        "col",
        scatter_dimension=0,
        tiled=True,
    )
    in_local = lax.dot_general(
        panel, dpre, (((0,), (0,)), ((), ())), preferred_element_type=jnp.float32
    )
    grad_in = (
        lax.psum_scatter(
            in_local.astype(jnp.bfloat16), "dp", scatter_dimension=1, tiled=True
        ).astype(jnp.float32)
        * factor
    )
    return (mixed, token_grad, grad_in, grad_out)


def solution(mesh):
    placed = (P(("col", "dp"), "row"), P(("col", "dp"), "row"), P("row", "col"), P("col", "row"))
    return jax.shard_map(
        shards,
        mesh=mesh,
        in_specs=placed,
        out_specs=(
            P(("col", "dp"), "row"),
            P(("col", "dp"), "row"),
            P("row", ("col", "dp")),
            P(("col", "dp"), "row"),
        ),
        check_vma=False,
    )
```

profile of v0, /device:TPU:0, one launch (start us, length us, event | category | flops | bytes accessed | tf_op | source)
XLA Modules:
  0.0 899.3 jit_solution(10898870089963239625)
XLA Ops:
  7.2 0.0 all-gather.9.cloned.1.call-start
  7.2 0.7 all-gather.9.cloned.1.call-update
  7.9 0.0 all-gather.5.cloned.1.call-start
  7.9 0.7 all-gather.5.cloned.1.call-update
  8.6 0.0 reduce-scatter.11.cloned.1.call-start
  8.7 56.6 %all-gather.9.cloned.1.call-done = bf16[1024,2048]{1,0:T(8,128)(2,1)} async-done(((bf16[256,2048]{1,0:T(8,128)(2,1)}), bf16[1024,2048]{1,0:T(8,128)(2,1)}) %all-gather.9.cloned.1.call-update) | async-done | bytes 4194320 | tf_op jit(solution)/shard_map/all_gather | solution.py:34
  65.3 22.9 %convolution_convert_fusion.1 = bf16[1024,4096]{1,0:T(8,128)(2,1)} fusion(bf16[1024,2048]{1,0:T(8,128)(2,1)} %all-gather.9.cloned.1.call-done, bf16[4096,2048]{1,0:T(8,128)(2,1)} %param.7), kind=kOutput, calls=%fused_computation.9 | convolution fusion | flops 17184063488 | bytes 29360128 | tf_op jit(solution)/shard_map/dot_general | solution.py:45
  88.2 0.0 reduce-scatter.11.cloned.1.call-update
  88.2 0.0 reduce-scatter.7.cloned.1.call-start
  88.3 31.6 %all-gather.5.cloned.1.call-done = bf16[1024,2048]{1,0:T(8,128)(2,1)} async-done(((bf16[256,2048]{1,0:T(8,128)(2,1)}), bf16[1024,2048]{1,0:T(8,128)(2,1)}) %all-gather.5.cloned.1.call-update) | async-done | bytes 4194320 | tf_op jit(solution)/shard_map/all_gather | solution.py:17
  119.9 22.8 %convolution_convert_fusion.2 = bf16[1024,4096]{1,0:T(8,128)(2,1)} fusion(bf16[1024,2048]{1,0:T(8,128)(2,1)} %all-gather.5.cloned.1.call-done, bf16[2048,4096]{1,0:T(8,128)(2,1)} %param.6), kind=kOutput, calls=%fused_computation.10 | convolution fusion | flops 17184063488 | bytes 29360128 | tf_op jit(solution)/shard_map/dot_general | solution.py:21
  142.7 0.0 reduce-scatter.7.cloned.1.call-update
  142.7 0.0 all-gather.11.cloned.1.call-start
  142.7 124.6 %reduce-scatter.11.cloned.1.call-done = bf16[256,4096]{1,0:T(8,128)(2,1)} async-done(((bf16[1024,4096]{1,0:T(8,128)(2,1)}), bf16[256,4096]{1,0:T(8,128)(2,1)}) %reduce-scatter.11.cloned.1.call-update) | async-done | bytes 2097168 | tf_op jit(solution)/shard_map/reduce_scatter | solution.py:44
  267.3 148.0 %reduce-scatter.7.cloned.1.call-done = bf16[256,4096]{1,0:T(8,128)(2,1)} async-done(((bf16[1024,4096]{1,0:T(8,128)(2,1)}), bf16[256,4096]{1,0:T(8,128)(2,1)}) %reduce-scatter.7.cloned.1.call-update) | async-done | bytes 2097168 | tf_op jit(solution)/shard_map/reduce_scatter | solution.py:20
  415.3 5.0 fusion.8
  420.4 0.0 all-gather.11.cloned.1.call-update
  420.4 0.0 all-gather.7.cloned.1.call-start
  420.4 0.5 all-gather.7.cloned.1.call-update
  421.0 0.2 reduce-scatter.15.cloned.1.call-start
  421.2 149.7 %all-gather.11.cloned.1.call-done = bf16[1024,4096]{1,0:T(8,128)(2,1)} async-done(((bf16[256,4096]{1,0:T(8,128)(2,1)}), bf16[1024,4096]{1,0:T(8,128)(2,1)}) %all-gather.11.cloned.1.call-update) | async-done | bytes 8388624 | tf_op jit(solution)/shard_map/all_gather | solution.py:52
  570.9 24.8 %convert_bitcast_fusion = bf16[2048,4096]{0,1:T(8,128)(2,1)} fusion(bf16[1024,4096]{1,0:T(8,128)(2,1)} %all-gather.11.cloned.1.call-done, bf16[1024,2048]{1,0:T(8,128)(2,1)} %all-gather.5.cloned.1.call-done), kind=kOutput, calls=%fused_computation.2 | convolution fusion | flops 17188257792 | bytes 29360128 | tf_op jit(solution)/shard_map/dot_general | solution.py:61
  595.7 0.0 reduce-scatter.15.cloned.1.call-update
  595.7 0.3 reduce-scatter.17.cloned.1.call-start
  596.0 124.8 %all-gather.7.cloned.1.call-done = bf16[1024,4096]{1,0:T(8,128)(2,1)} async-done(((bf16[256,4096]{1,0:T(8,128)(2,1)}), bf16[1024,4096]{1,0:T(8,128)(2,1)}) %all-gather.7.cloned.1.call-update) | async-done | bytes 8388624 | tf_op jit(solution)/shard_map/all_gather | solution.py:27
  720.8 26.2 %convolution_convert_fusion = bf16[4096,2048]{0,1:T(8,128)(2,1)} fusion(bf16[1024,4096]{1,0:T(8,128)(2,1)} %all-gather.7.cloned.1.call-done, bf16[1024,2048]{1,0:T(8,128)(2,1)} %all-gather.9.cloned.1.call-done), kind=kOutput, calls=%fused_computation.3 | convolution fusion | flops 17188257792 | bytes 29360128 | tf_op jit(solution)/shard_map/dot_general | solution.py:35
  747.0 0.0 reduce-scatter.17.cloned.1.call-update
  747.0 0.0 reduce-scatter.9.cloned.1.call-start
  747.1 23.9 %convolution_convert_fusion.4 = bf16[1024,2048]{1,0:T(8,128)(2,1)} fusion(bf16[1024,4096]{1,0:T(8,128)(2,1)} %all-gather.7.cloned.1.call-done, bf16[4096,2048]{1,0:T(8,128)(2,1)} %param.7), kind=kOutput, calls=%fused_computation.21 | convolution fusion | flops 17181966336 | bytes 29360128 | tf_op jit(solution)/shard_map/dot_general | solution.py:29
  771.0 0.0 reduce-scatter.9.cloned.1.call-update
  771.0 0.3 reduce-scatter.13.cloned.1.call-start
  771.3 26.1 %convolution_convert_fusion.3 = bf16[1024,2048]{1,0:T(8,128)(2,1)} fusion(bf16[1024,4096]{1,0:T(8,128)(2,1)} %all-gather.11.cloned.1.call-done, bf16[2048,4096]{1,0:T(8,128)(2,1)} %param.6), kind=kOutput, calls=%fused_computation.20 | convolution fusion | flops 17181966336 | bytes 29360128 | tf_op jit(solution)/shard_map/dot_general | solution.py:54
  797.4 0.0 reduce-scatter.13.cloned.1.call-update
  797.4 0.0 reduce-scatter.15.cloned.1.call-done
  797.4 12.3 %convert_multiply_fusion.1 = f32[2048,2048]{0,1:T(8,128)} fusion(bf16[2048,2048]{0,1:T(8,128)(2,1)} %reduce-scatter.15.cloned.1.call-done), kind=kLoop, calls=%fused_computation.1 | loop fusion | flops 8388608 | bytes 25165824 | tf_op jit(solution)/shard_map/mul | solution.py:65
  809.7 17.7 %copy.9 = f32[2048,2048]{1,0:T(8,128)} copy(f32[2048,2048]{0,1:T(8,128)} %convert_multiply_fusion.1) | data formatting | bytes 33554432
  827.3 0.0 reduce-scatter.17.cloned.1.call-done
  827.3 11.6 %convert_multiply_fusion = f32[2048,2048]{0,1:T(8,128)} fusion(bf16[2048,2048]{0,1:T(8,128)(2,1)} %reduce-scatter.17.cloned.1.call-done), kind=kLoop, calls=%fused_computation | loop fusion | flops 8388608 | bytes 25165824 | tf_op jit(solution)/shard_map/mul | solution.py:39
  838.9 17.8 %copy.10 = f32[2048,2048]{1,0:T(8,128)} copy(f32[2048,2048]{0,1:T(8,128)} %convert_multiply_fusion) | data formatting | bytes 33554432
  856.8 0.0 reduce-scatter.9.cloned.1.call-done
  856.8 35.2 %reduce-scatter.13.cloned.1.call-done = bf16[256,2048]{1,0:T(8,128)(2,1)} async-done(((bf16[1024,2048]{1,0:T(8,128)(2,1)}), bf16[256,2048]{1,0:T(8,128)(2,1)}) %reduce-scatter.13.cloned.1.call-update) | async-done | bytes 1048592 | tf_op jit(solution)/shard_map/reduce_scatter | solution.py:53
Async XLA Ops:
  7.2 58.1 %all-gather.9.cloned.1.call-start = ((), (), s32[]{:S(2)}) async-start(), calls=%async_computation.10 | async-start | bytes 5242880 | tf_op jit(solution)/shard_map/all_gather | solution.py:34
  7.9 112.0 %all-gather.5.cloned.1.call-start = ((), (), s32[]{:S(2)}) async-start(), calls=%async_computation.6 | async-start | bytes 5242880 | tf_op jit(solution)/shard_map/all_gather | solution.py:17
  8.6 258.6 %reduce-scatter.11.cloned.1.call-start = ((), (), s32[]{:S(2)}) async-start(), calls=%async_computation.11 | async-start | bytes 10485760 | tf_op jit(solution)/shard_map/reduce_scatter | solution.py:44
  88.2 327.1 %reduce-scatter.7.cloned.1.call-start = ((), (), s32[]{:S(2)}) async-start(), calls=%async_computation.7 | async-start | bytes 10485760 | tf_op jit(solution)/shard_map/reduce_scatter | solution.py:20
  142.7 428.2 %all-gather.11.cloned.1.call-start = ((), (), s32[]{:S(2)}) async-start(), calls=%async_computation.12 | async-start | bytes 10485760 | tf_op jit(solution)/shard_map/all_gather | solution.py:52
  420.4 300.4 %all-gather.7.cloned.1.call-start = ((), (), s32[]{:S(2)}) async-start(), calls=%async_computation.8 | async-start | bytes 10485760 | tf_op jit(solution)/shard_map/all_gather | solution.py:27
  421.0 376.4 %reduce-scatter.15.cloned.1.call-start = ((), (), s32[]{:S(2)}) async-start(), calls=%async_computation.14 | async-start | bytes 25165824 | tf_op jit(solution)/shard_map/reduce_scatter | solution.py:65
  595.7 231.6 %reduce-scatter.17.cloned.1.call-start = ((), (), s32[]{:S(2)}) async-start(), calls=%async_computation.15 | async-start | bytes 25165824 | tf_op jit(solution)/shard_map/reduce_scatter | solution.py:39
  747.0 109.7 %reduce-scatter.9.cloned.1.call-start = ((), (), s32[]{:S(2)}) async-start(), calls=%async_computation.9 | async-start | bytes 5242880 | tf_op jit(solution)/shard_map/reduce_scatter | solution.py:28
  771.0 121.0 %reduce-scatter.13.cloned.1.call-start = ((), (), s32[]{:S(2)}) async-start(), calls=%async_computation.13 | async-start | bytes 5242880 | tf_op jit(solution)/shard_map/reduce_scatter | solution.py:53
Sparse Core Ops, SparseCore 0:
  9.8 55.3 all-gather.8
  67.1 52.6 all-gather.4
  122.8 144.4 reduce-scatter.10
  270.1 145.1 reduce-scatter.6
  420.5 150.3 all-gather.10
  572.9 147.8 all-gather.6
  723.7 24.4 reduce-scatter.14
  750.6 27.5 reduce-scatter.16
  781.7 53.8 reduce-scatter.8
  839.3 52.6 reduce-scatter.12
where the time goes:
time: 906 us; the launch traced here: 899 us
  waiting for transfers between devices  673 us (74%)
  matrix products  147 us (16%)
  local copies, waits for them, and re-layouts  35.5 us (4%)
  other arithmetic  28.9 us (3%)
  between operations  14.6 us (2%)
    all_gather x1, waiting for transfers between devices, shards(): lax.all_gather((back * slope).astype(jnp.bfloat16), 'row', axis=0, tiled=...  150 us
    reduce_scatter x1, waiting for transfers between devices, shards(): lax.psum_scatter(jnp.dot(panel, weight_in, preferred_element_type=jnp.flo...  148 us
    all_gather x1, waiting for transfers between devices, shards(): lax.all_gather(activated.astype(jnp.bfloat16), 'row', axis=0, tiled=True)  125 us
    reduce_scatter x1, waiting for transfers between devices, shards(): lax.psum_scatter(lax.dot_general(grad_panel, weight_out, (((1,), (1,)), (...  125 us
    all_gather x1, waiting for transfers between devices, shards(): grad_panel = lax.all_gather(out_grad, 'col', axis=0, tiled=True)  56.6 us
    unnamed x2, local copies, waits for them, and re-layouts  35.5 us
    reduce_scatter x1, waiting for transfers between devices, shards(): lax.psum_scatter(lax.dot_general(dpre, weight_in, (((1,), (1,)), ((), ())...  35.2 us
    all_gather x1, waiting for transfers between devices, shards(): panel = lax.all_gather(tokens, 'col', axis=0, tiled=True)  31.6 us
  transfers between devices with their start and end apart: 10, of which 7 were waited for; matrix products, arithmetic and copies ran while one was open for 23% of the time, Pallas kernels for 0%

commit v1 on v0

v1 whole, which is shorter than its diff:
```python
import math

import jax
import jax.numpy as jnp
from jax import lax
from jax.sharding import PartitionSpec as P

F32, BF16 = jnp.float32, jnp.bfloat16


def gelu_parts(pre):
    cdf = 0.5 * (1.0 + jax.scipy.special.erf(pre * (1.0 / math.sqrt(2.0))))
    activated = pre * cdf
    slope = cdf + pre * jnp.exp(-0.5 * pre * pre) * (1.0 / math.sqrt(2.0 * math.pi))
    return (activated, slope)


class LineSum:
    def __init__(self, axis):
        self.axis = axis
        self.size = lax.axis_size(axis)
        self.me = lax.axis_index(axis)
        self.moving = None
        self.gathered = None
        self.pending = None

    def shift(self, pair):
        n = self.size
        right = [(i, i + 1) for i in range(n - 1)]
        left = [(i + 1, i) for i in range(n - 1)]
        return (lax.ppermute(pair[0], self.axis, right), lax.ppermute(pair[1], self.axis, left))

    def tick(self, s, parts):
        n, z = self.size, self.me
        sends = []
        for direction in range(2):
            at = z if direction == 0 else n - 1 - z
            send = None if self.moving is None else self.moving[direction]
            if parts is not None:
                shard = jnp.clip(n - s + at, 0, n - 1)
                shard = shard if direction == 0 else n - 1 - shard
                own = lax.dynamic_index_in_dim(parts, shard, 0, keepdims=False)
                own = jnp.where(at < s, own, jnp.zeros_like(own))
                send = own if send is None else (send.astype(F32) + own.astype(F32)).astype(BF16)
            sends.append(send)
        self.moving = self.shift(sends)
        if self.pending is not None and s <= n - 2:
            self.gathered.append(self.moving)

    def collect(self):
        n, z = self.size, self.me
        own, got = self.pending, self.gathered
        full = jnp.zeros((n,) + own.shape, own.dtype)
        full = lax.dynamic_update_index_in_dim(full, own, z, 0)
        for a in range(1, n):
            piece = jnp.where(z >= a, got[a - 1][0], got[n - a - 1][1])
            full = lax.dynamic_update_index_in_dim(full, piece, lax.rem(z - a + n, n), 0)
        return full.reshape((-1,) + own.shape[1:])

    def steps(self, parts, finish):
        n = self.size
        for s in range(1, n):
            self.tick(s, parts)
            if s == max(n - 2, 1) and self.pending is not None:
                yield self.collect()
            else:
                yield None
        if parts is None:
            return
        own = lax.dynamic_index_in_dim(parts, self.me, 0, keepdims=False).astype(F32)
        total = own + self.moving[0].astype(F32) + self.moving[1].astype(F32)
        self.pending = finish(total)
        self.moving = self.shift((self.pending, self.pending))
        self.gathered = [self.moving]
        yield None

    def drain(self):
        n = self.size
        for s in range(1, n - 1):
            self.moving = self.shift(self.moving)
            self.gathered.append(self.moving)
            yield None
        yield self.collect()


def shards(tokens, out_grad, weight_in, weight_out):
    cols = lax.axis_size("col")
    rows = lax.axis_size("row")
    factor = 1.0 / math.sqrt(tokens.shape[0] * cols * lax.axis_size("dp"))
    hidden = weight_in.shape[1]
    half = hidden // 2
    core = lax.axis_index("dp")

    def swap(x, k):
        return x if k == 0 else lax.ppermute(x, "col", [(i, i ^ k) for i in range(cols)])

    def other(x):
        return lax.ppermute(x, "dp", [(0, 1), (1, 0)])

    def both(x):
        mine = lax.dynamic_slice_in_dim(x, core * half, half, 1)
        theirs = lax.dynamic_slice_in_dim(x, (1 - core) * half, half, 1)
        return [mine, other(theirs)]

    def cut(x):
        return x.astype(BF16).reshape(rows, -1, hidden)

    tok = [swap(tokens, k) for k in range(cols)]
    cot = [swap(out_grad, k) for k in range(cols)]
    tok_all = [(t, other(t)) for t in tok]
    cot_all = [(t, other(t)) for t in cot]

    slopes, act, dpre = {}, {}, {}
    mixed_parts, token_parts = {}, {}

    def forward(k):
        parts = cut(jnp.dot(tok[k], weight_in, preferred_element_type=F32))

        def finish(total):
            activated, slopes[k] = gelu_parts(total)
            return activated.astype(BF16)

        return parts, finish

    def backward(k):
        parts = cut(
            lax.dot_general(cot[k], weight_out, (((1,), (1,)), ((), ())), preferred_element_type=F32)
        )
        return parts, lambda total: (total * slopes[k]).astype(BF16)

    def done(kind, k, block):
        if kind == 0:
            act[k] = both(block)
            part = jnp.dot(block, weight_out, preferred_element_type=F32)
            mixed_parts[k] = swap(part.astype(BF16), k)
        else:
            dpre[k] = both(block)
            part = lax.dot_general(
                block, weight_in, (((1,), (1,)), ((), ())), preferred_element_type=F32
            )
            token_parts[k] = swap(part.astype(BF16), k)

    def chain(first):
        line = LineSum("row")
        last = None
        for kind in range(2):
            for k in range(first, cols, 2):
                parts, finish = (forward, backward)[kind](k)
                for block in line.steps(parts, finish):
                    if block is not None:
                        done(*last, block)
                    yield
                last = (kind, k)
        for block in line.drain():
            if block is not None:
                done(*last, block)
            yield

    running = [chain(first) for first in range(min(2, cols))]
    while running:
        still = []
        for one in running:
            try:
                next(one)
                still.append(one)
            except StopIteration:
                pass
        running = still

    def summed(parts):
        total = parts[0].astype(F32)
        for k in range(1, cols):
            total = total + parts[k].astype(F32)
        return total.astype(BF16)

    def joined(pairs, ks):
        return jnp.concatenate([x for k in ks for x in pairs[k]], axis=0)

    def across(left, right):
        return lax.dot_general(left, right, (((0,), (0,)), ((), ())), preferred_element_type=F32)

    every = range(cols)
    grad_out = across(joined(act, every), joined(cot_all, every)) * factor
    early, late = range(cols // 2), range(cols // 2, cols)
    grad_in = across(joined(tok_all, early), joined(dpre, early))
    grad_in = (grad_in + across(joined(tok_all, late), joined(dpre, late))) * factor
    return (summed(mixed_parts), summed(token_parts), grad_in, grad_out)


def solution(mesh):
    placed = (P(("col", "dp"), "row"), P(("col", "dp"), "row"), P("row", "col"), P("col", "row"))
    return jax.shard_map(
        shards,
        mesh=mesh,
        in_specs=placed,
        out_specs=(
            P(("col", "dp"), "row"),
            P(("col", "dp"), "row"),
            P("row", ("col", "dp")),
            P(("col", "dp"), "row"),
        ),
        check_vma=False,
    )
```

time: 906 us -> 694 us (0.77)
  waiting for transfers between devices: 673 us -> 171 us
  starting transfers between devices: 1.04 us -> 218 us
  matrix products: 147 us -> 223 us
  between operations: 14.6 us -> 2.52 us
    all_gather x4 -> x0, waiting for transfers between devices: 363 us -> none  [the longest x1 150 us: shards(): lax.all_gather((back * slope).astype(jnp.bfloat16), 'row', axis=0, tiled=...]
    reduce_scatter x6 -> x0, waiting for transfers between devices: 308 us -> none  [the longest x1 148 us: shards(): lax.psum_scatter(jnp.dot(panel, weight_in, preferred_element_type=jnp.flo...]
    ppermute x0 -> x100, starting transfers between devices: none -> 218 us  [the longest x36 155 us: shift(): lax.ppermute(pair[0], self.axis, right)]
    ppermute x0 -> x100, waiting for transfers between devices: none -> 171 us  [the longest x36 97.4 us: shift(): lax.ppermute(pair[1], self.axis, left)]
    dot_general x6 -> x19, matrix products: 147 us -> 223 us  [the longest x3 57.9 us: across(): lax.dot_general(left, right, (((0,), (0,)), ((), ())), preferred_element_...]
    mul x2 -> x0, other arithmetic: 23.9 us -> none  [the longest x1 12.3 us: shards(): lax.psum_scatter(in_local.astype(jnp.bfloat16), 'dp', scatter_dimension=1...]
    dynamic_update_slice x0 -> x32, other arithmetic: none -> 17 us  [the longest x24 9.81 us: collect(): lax.dynamic_update_index_in_dim(full, piece, lax.rem(z - a + n, n), 0)]
    unnamed x2 -> x62, local copies, waits for them, and re-layouts: 35.5 us -> 21.8 us
  transfers between devices with their start and end apart: 10 -> 100, of which waited for: 7 -> 40; matrix products, arithmetic and copies ran while one was open for 23% -> 39% of each run, Pallas kernels for 0% -> 0%
where the time goes in v1:
time: 694 us; the launch traced here: 684 us
  matrix products  223 us (32%)
  starting transfers between devices  218 us (31%)
  waiting for transfers between devices  171 us (25%)
  local copies, waits for them, and re-layouts  39.5 us (6%)
  other arithmetic  29.5 us (4%)
    ppermute x36, starting transfers between devices, shift(): lax.ppermute(pair[0], self.axis, right)  155 us
    ppermute x36, waiting for transfers between devices, shift(): lax.ppermute(pair[1], self.axis, left)  97.4 us
    ppermute x36, waiting for transfers between devices, shift(): lax.ppermute(pair[0], self.axis, right)  74 us
    dot_general x3, matrix products, across(): lax.dot_general(left, right, (((0,), (0,)), ((), ())), preferred_element_...  57.9 us
    dot_general x4, matrix products, backward(): lax.dot_general(cot[k], weight_out, (((1,), (1,)), ((), ())), preferred_e...  47.8 us
    ppermute x36, starting transfers between devices, shift(): lax.ppermute(pair[1], self.axis, left)  47.1 us
    dot_general x4, matrix products, done(): lax.dot_general(block, weight_in, (((1,), (1,)), ((), ())), preferred_ele...  44.2 us
    dot_general x4, matrix products, done(): part = jnp.dot(block, weight_out, preferred_element_type=F32)  37.8 us
  transfers between devices with their start and end apart: 100, of which 40 were waited for; matrix products, arithmetic and copies ran while one was open for 39% of the time, Pallas kernels for 0%

profile of v1, /device:TPU:0, one launch (start us, length us, event | category | flops | bytes accessed | tf_op | source)
XLA Modules:
  0.0 684.4 jit_solution(998100843211314202)
XLA Ops:
  5.2 10.6 %convolution_convert_fusion.7 = bf16[256,4096]{1,0:T(8,128)(2,1)S(1)} fusion(bf16[256,2048]{1,0:T(8,128)(2,1)} %param.4, bf16[2048,4096]{1,0:T(8,128)(2,1)} %param.6), kind=kOutput, calls=%fused_computation.9 | convolution fusion | flops 4296015872 | bytes 19922944 | tf_op jit(solution)/shard_map/dot_general | solution.py:117
  15.9 4.8 collective-permute-start
  21.9 11.9 %convolution_convert_fusion.3 = bf16[256,4096]{1,0:T(8,128)(2,1)} fusion(bf16[256,2048]{1,0:T(8,128)(2,1)} %param.5, bf16[4096,2048]{1,0:T(8,128)(2,1)} %param.7), kind=kOutput, calls=%fused_computation.5 | convolution fusion | flops 4296015872 | bytes 19922944 | tf_op jit(solution)/shard_map/dot_general | solution.py:127
  40.8 5.2 collective-permute-start.1
  46.0 11.9 %convolution_convert_fusion.6 = bf16[256,4096]{1,0:T(8,128)(2,1)} fusion(bf16[256,2048]{1,0:T(8,128)(2,1)} %collective-permute-done.8, bf16[2048,4096]{1,0:T(8,128)(2,1)} %param.6), kind=kOutput, calls=%fused_computation.8 | convolution fusion | flops 4296015872 | bytes 19922944 | tf_op jit(solution)/shard_map/dot_general | solution.py:117
  59.3 5.9 convolution_convert_fusion.5
  66.9 4.5 collective-permute-done.4
  73.9 6.9 %convolution_convert_fusion.4 = bf16[256,4096]{1,0:T(8,128)(2,1)} fusion(bf16[256,2048]{1,0:T(8,128)(2,1)} %collective-permute-done.22, bf16[2048,4096]{1,0:T(8,128)(2,1)S(1)} %bitcast.381), kind=kOutput, calls=%fused_computation.6 | convolution fusion | flops 4296015872 | bytes 19922944 | tf_op jit(solution)/shard_map/dot_general | solution.py:117
  80.9 5.0 collective-permute-start.2
  85.9 12.0 %convolution_convert_fusion.2 = bf16[256,4096]{1,0:T(8,128)(2,1)} fusion(bf16[256,2048]{1,0:T(8,128)(2,1)} %collective-permute-done.41, bf16[4096,2048]{1,0:T(8,128)(2,1)} %param.7), kind=kOutput, calls=%fused_computation.4 | convolution fusion | flops 4296015872 | bytes 19922944 | tf_op jit(solution)/shard_map/dot_general | solution.py:127
  97.9 4.1 collective-permute-start.14
  101.9 12.0 %convolution_convert_fusion.1 = bf16[256,4096]{1,0:T(8,128)(2,1)} fusion(bf16[256,2048]{1,0:T(8,128)(2,1)} %collective-permute-done.51, bf16[4096,2048]{1,0:T(8,128)(2,1)} %param.7), kind=kOutput, calls=%fused_computation.3 | convolution fusion | flops 4296015872 | bytes 19922944 | tf_op jit(solution)/shard_map/dot_general | solution.py:127
  115.4 11.9 %convolution_convert_fusion = bf16[256,4096]{1,0:T(8,128)(2,1)} fusion(bf16[256,2048]{1,0:T(8,128)(2,1)} %collective-permute-done.60, bf16[4096,2048]{1,0:T(8,128)(2,1)} %param.7), kind=kOutput, calls=%fused_computation.2 | convolution fusion | flops 4296015872 | bytes 19922944 | tf_op jit(solution)/shard_map/dot_general | solution.py:127
  133.4 4.7 collective-permute-start.6
  141.0 8.8 %collective-permute-done.6 = bf16[64,4096]{1,0:T(8,128)(2,1)S(1)} collective-permute-done((bf16[64,4096]{1,0:T(8,128)(2,1)S(1)}, bf16[64,4096]{1,0:T(8,128)(2,1)S(1)}, u32[]{:S(2)}, u32[]{:S(2)}) %collective-permute-start.6) | collective-permute-done | bytes 524320 | tf_op jit(solution)/shard_map/ppermute | solution.py:31
  149.8 4.4 collective-permute-start.15
  155.8 9.2 %collective-permute-done.15 = bf16[64,4096]{1,0:T(8,128)(2,1)S(1)} collective-permute-done((bf16[64,4096]{1,0:T(8,128)(2,1)S(1)}, bf16[64,4096]{1,0:T(8,128)(2,1)S(1)}, u32[]{:S(2)}, u32[]{:S(2)}) %collective-permute-start.15) | collective-permute-done | bytes 524320 | tf_op jit(solution)/shard_map/ppermute | solution.py:31
  165.1 4.4 collective-permute-start.11
  175.8 5.2 collective-permute-start.16
  185.6 9.2 %collective-permute-done.19 = bf16[64,4096]{1,0:T(8,128)(2,1)S(1)} collective-permute-done((bf16[64,4096]{1,0:T(8,128)(2,1)S(1)}, bf16[64,4096]{1,0:T(8,128)(2,1)S(1)}, u32[]{:S(2)}, u32[]{:S(2)}) %collective-permute-start.19) | collective-permute-done | bytes 524320 | tf_op jit(solution)/shard_map/ppermute | solution.py:31
  201.4 5.2 collective-permute-start.12
  206.6 4.2 collective-permute-done.20
  210.8 4.4 collective-permute-done.21
  219.5 6.9 %collective-permute-done.10 = bf16[64,4096]{1,0:T(8,128)(2,1)S(1)} collective-permute-done((bf16[64,4096]{1,0:T(8,128)(2,1)S(1)}, bf16[64,4096]{1,0:T(8,128)(2,1)S(1)}, u32[]{:S(2)}, u32[]{:S(2)}) %collective-permute-start.10) | collective-permute-done | bytes 524320 | tf_op jit(solution)/shard_map/ppermute | solution.py:31
  228.1 4.6 collective-permute-start.28
  242.0 6.0 collective-permute-done.29
  255.1 4.1 collective-permute-done.24
  260.9 4.6 collective-permute-start.37
  266.3 4.1 collective-permute-done.31
  275.7 9.2 %convolution_convert_fusion.14 = bf16[256,2048]{1,0:T(8,128)(2,1)} fusion(bf16[256,4096]{1,0:T(8,128)(2,1)S(1)} %bitcast.338, bf16[4096,2048]{1,0:T(8,128)(2,1)} %param.7), kind=kOutput, calls=%fused_computation.49 | convolution fusion | flops 4295491584 | bytes 19922944 | tf_op jit(solution)/shard_map/dot_general | solution.py:134
  288.4 4.7 collective-permute-start.39
  296.1 8.9 %collective-permute-done.39 = bf16[64,4096]{1,0:T(8,128)(2,1)S(1)} collective-permute-done((bf16[64,4096]{1,0:T(8,128)(2,1)S(1)}, bf16[64,4096]{1,0:T(8,128)(2,1)S(1)}, u32[]{:S(2)}, u32[]{:S(2)}) %collective-permute-start.39) | collective-permute-done | bytes 524320 | tf_op jit(solution)/shard_map/ppermute | solution.py:31
  305.0 4.4 collective-permute-start.35
  312.5 7.9 %collective-permute-done.33 = bf16[64,4096]{1,0:T(8,128)(2,1)S(1)} collective-permute-done((bf16[64,4096]{1,0:T(8,128)(2,1)S(1)}, bf16[64,4096]{1,0:T(8,128)(2,1)S(1)}, u32[]{:S(2)}, u32[]{:S(2)}) %collective-permute-start.33) | collective-permute-done | bytes 524320 | tf_op jit(solution)/shard_map/ppermute | solution.py:31
  322.1 9.2 %convolution_convert_fusion.13 = bf16[256,2048]{1,0:T(8,128)(2,1)} fusion(bf16[256,4096]{1,0:T(8,128)(2,1)S(1)} %bitcast.340, bf16[4096,2048]{1,0:T(8,128)(2,1)} %param.7), kind=kOutput, calls=%fused_computation.48 | convolution fusion | flops 4295491584 | bytes 19922944 | tf_op jit(solution)/shard_map/dot_general | solution.py:134
  335.8 5.2 collective-permute-start.47
  341.4 6.2 collective-permute-done.48
  351.1 4.4 collective-permute-start.45
  356.6 5.0 collective-permute-done.43
  369.3 9.4 %convolution_convert_fusion.12 = bf16[256,2048]{1,0:T(8,128)(2,1)} fusion(bf16[256,4096]{1,0:T(8,128)(2,1)S(1)} %bitcast.342, bf16[4096,2048]{1,0:T(8,128)(2,1)} %param.7), kind=kOutput, calls=%fused_computation.47 | convolution fusion | flops 4295491584 | bytes 19922944 | tf_op jit(solution)/shard_map/dot_general | solution.py:134
  381.4 5.0 collective-permute-start.54
  394.4 8.3 %collective-permute-done.52 = bf16[64,4096]{1,0:T(8,128)(2,1)S(1)} collective-permute-done((bf16[64,4096]{1,0:T(8,128)(2,1)S(1)}, bf16[64,4096]{1,0:T(8,128)(2,1)S(1)}, u32[]{:S(2)}, u32[]{:S(2)}) %collective-permute-start.52) | collective-permute-done | bytes 524320 | tf_op jit(solution)/shard_map/ppermute | solution.py:31
  411.5 7.0 %collective-permute-done.56 = bf16[64,4096]{1,0:T(8,128)(2,1)S(1)} collective-permute-done((bf16[64,4096]{1,0:T(8,128)(2,1)S(1)}, bf16[64,4096]{1,0:T(8,128)(2,1)S(1)}, u32[]{:S(2)}, u32[]{:S(2)}) %collective-permute-start.56) | collective-permute-done | bytes 524320 | tf_op jit(solution)/shard_map/ppermute | solution.py:31
  418.5 4.4 collective-permute-start.55
  435.5 5.9 collective-permute-done.59
  441.8 4.0 collective-permute-start.63
  448.4 9.9 %fusion.37 = bf16[256,2048]{1,0:T(8,128)(2,1)} fusion(bf16[256,4096]{1,0:T(8,128)(2,1)S(1)} %bitcast.337, bf16[4096,2048]{1,0:T(8,128)(2,1)} %param.7, bf16[256,2048]{1,0:T(8,128)(2,1)S(1)} %collective-permute-done.46, bf16[256,2048]{1,0:T(8,128)(2,1)S(1)} %collective-permute-done.36, bf16[256,2048]{1,0:T(8,128)(2,1)} %collective-permute-done.27), kind=kOutput, calls=%fused_computation.55 | convolution fusion | flops 4299685888 | bytes 23068672 | tf_op jit(solution)/shard_map/dot_general | solution.py:134
  460.3 5.2 collective-permute-start.66
  472.9 4.9 collective-permute-done.66
  481.1 5.2 collective-permute-start.68
  491.6 5.8 collective-permute-start.75
  497.4 5.9 collective-permute-done.69
  505.2 10.0 %convolution_convert_fusion.10 = bf16[256,2048]{1,0:T(8,128)(2,1)} fusion(bf16[256,4096]{1,0:T(8,128)(2,1)S(1)} %bitcast.334, bf16[2048,4096]{1,0:T(8,128)(2,1)} %param.6), kind=kOutput, calls=%fused_computation.41 | convolution fusion | flops 4295491584 | bytes 19922944 | tf_op jit(solution)/shard_map/dot_general | solution.py:138
  515.3 4.6 collective-permute-start.72
  526.4 4.6 collective-permute-start.77
  549.3 5.0 collective-permute-done.73
  554.4 5.2 collective-permute-start.81
  563.8 11.9 %convolution_convert_fusion.9 = bf16[256,2048]{1,0:T(8,128)(2,1)} fusion(bf16[256,4096]{1,0:T(8,128)(2,1)} %bitcast.95, bf16[2048,4096]{1,0:T(8,128)(2,1)} %param.6), kind=kOutput, calls=%fused_computation.40 | convolution fusion | flops 4295491584 | bytes 19922944 | tf_op jit(solution)/shard_map/dot_general | solution.py:138
  583.4 7.0 %collective-permute-done.82 = bf16[64,4096]{1,0:T(8,128)(2,1)S(1)} collective-permute-done((bf16[64,4096]{1,0:T(8,128)(2,1)}, bf16[64,4096]{1,0:T(8,128)(2,1)S(1)}, u32[]{:S(2)}, u32[]{:S(2)}) %collective-permute-start.82) | collective-permute-done | bytes 524320 | tf_op jit(solution)/shard_map/ppermute | solution.py:31
  590.5 9.2 %convolution_convert_fusion.8 = bf16[256,2048]{1,0:T(8,128)(2,1)} fusion(bf16[256,4096]{1,0:T(8,128)(2,1)S(1)} %bitcast.330, bf16[2048,4096]{1,0:T(8,128)(2,1)} %param.6), kind=kOutput, calls=%fused_computation.39 | convolution fusion | flops 4295491584 | bytes 19922944 | tf_op jit(solution)/shard_map/dot_general | solution.py:138
  601.3 24.6 %convolution_multiply_fusion = f32[2048,2048]{1,0:T(8,128)} fusion(bf16[2048,2048]{1,0:T(8,128)(2,1)} %constant_dynamic-update-slice_fusion, bf16[2048,2048]{1,0:T(8,128)(2,1)} %constant_dynamic-update-slice_fusion.4), kind=kOutput, calls=%fused_computation.1 | convolution fusion | flops 17184063488 | bytes 33554432 | tf_op jit(solution)/shard_map/dot_general | solution.py:180
  633.2 13.1 %fusion.38 = bf16[256,2048]{1,0:T(8,128)(2,1)} fusion(bf16[256,4096]{1,0:T(8,128)(2,1)} %bitcast.333, bf16[2048,4096]{1,0:T(8,128)(2,1)} %param.6, bf16[256,2048]{1,0:T(8,128)(2,1)} %copy-done.19, bf16[256,2048]{1,0:T(8,128)(2,1)} %collective-permute-done.74, bf16[256,2048]{1,0:T(8,128)(2,1)} %collective-permute-done.65), kind=kOutput, calls=%fused_computation.56 | convolution fusion | flops 4299685888 | bytes 23068672 | tf_op jit(solution)/shard_map/dot_general | solution.py:138
  647.6 15.5 %fusion.14 = f32[2048,2048]{1,0:T(8,128)} fusion(bf16[256,2048]{1,0:T(8,128)(2,1)} %collective-permute-done.89, bf16[256,2048]{1,0:T(8,128)(2,1)} %collective-permute-done.22, bf16[256,2048]{1,0:T(8,128)(2,1)} %copy-done.17, bf16[256,2048]{1,0:T(8,128)(2,1)} %collective-permute-done.8, bf16[256,2048]{1,0:T(8,128)(2,1)} %collective-permute-done.91, ...), kind=kOutput, calls=%fused_computation.24 | convolution fusion | flops 8623489024 | bytes 25165824 | tf_op jit(solution)/shard_map/dot_general | solution.py:180
  666.1 17.9 %add_multiply_fusion = f32[2048,2048]{1,0:T(8,128)} fusion(f32[2048,2048]{1,0:T(8,128)} %fusion.14, bf16[256,2048]{1,0:T(8,128)(2,1)} %copy-done.18, bf16[256,2048]{1,0:T(8,128)(2,1)} %collective-permute-done.13, bf16[256,2048]{1,0:T(8,128)(2,1)} %collective-permute-done.84, bf16[256,2048]{1,0:T(8,128)(2,1)} %param.4, bf16[256,2048]{1,0:T(8,128)(2,1)} %copy-done.21, ...), kind=kOutput, calls=%fused_computation | convolution fusion | flops 8631877632 | bytes 41943040 | tf_op jit(solution)/shard_map/dot_general | solution.py:180
  (292 shorter events, 210.6 us)
Async XLA Ops:
  0.6 40.1 %collective-permute-start.8 = (bf16[256,2048]{1,0:T(8,128)(2,1)}, bf16[256,2048]{1,0:T(8,128)(2,1)}, u32[]{:S(2)}, u32[]{:S(2)}) collective-permute-start(bf16[256,2048]{1,0:T(8,128)(2,1)} %param.4), channel_id=1, source_target_pairs={{0,4},{2,6},{4,0},{6,2},{1,5},{3,7},{5,1},{7,3},{8,12},{10,14},{12... | collective-permute-start | bytes 3145736 | tf_op jit(solution)/shard_map/ppermute | solution.py:95
  3.7 54.3 %collective-permute-start.13 = (bf16[256,2048]{1,0:T(8,128)(2,1)}, bf16[256,2048]{1,0:T(8,128)(2,1)}, u32[]{:S(2)}, u32[]{:S(2)}) collective-permute-start(bf16[256,2048]{1,0:T(8,128)(2,1)} %param.4), channel_id=1, source_target_pairs={{0,2},{2,0},{4,6},{6,4},{1,3},{3,1},{5,7},{7,5},{8,10},{10,8},{12,... | collective-permute-start | bytes 3145736 | tf_op jit(solution)/shard_map/ppermute | solution.py:95
  5.2 67.5 %collective-permute-start.22 = (bf16[256,2048]{1,0:T(8,128)(2,1)}, bf16[256,2048]{1,0:T(8,128)(2,1)}, u32[]{:S(2)}, u32[]{:S(2)}) collective-permute-start(bf16[256,2048]{1,0:T(8,128)(2,1)} %param.4), channel_id=1, source_target_pairs={{0,6},{2,4},{4,2},{6,0},{1,7},{3,5},{5,3},{7,1},{8,14},{10,12},{12... | collective-permute-start | bytes 3145736 | tf_op jit(solution)/shard_map/ppermute | solution.py:95
  15.9 20.3 %collective-permute-start = (bf16[64,4096]{1,0:T(8,128)(2,1)S(1)}, bf16[64,4096]{1,0:T(8,128)(2,1)}, u32[]{:S(2)}, u32[]{:S(2)}) collective-permute-start(bf16[64,4096]{1,0:T(8,128)(2,1)S(1)} %get-tuple-element.82), channel_id=1, source_target_pairs={{0,8},{8,16},{16,24},{1,9},{9,17},{17,25},{2,10},{10,18},{18,26},{... | collective-permute-start | bytes 1572872 | tf_op jit(solution)/shard_map/ppermute | solution.py:31
  36.2 44.7 %collective-permute-start.41 = (bf16[256,2048]{1,0:T(8,128)(2,1)}, bf16[256,2048]{1,0:T(8,128)(2,1)}, u32[]{:S(2)}, u32[]{:S(2)}) collective-permute-start(bf16[256,2048]{1,0:T(8,128)(2,1)} %param.5), channel_id=1, source_target_pairs={{0,2},{2,0},{4,6},{6,4},{1,3},{3,1},{5,7},{7,5},{8,10},{10,8},{12,... | collective-permute-start | bytes 3145736 | tf_op jit(solution)/shard_map/ppermute | solution.py:95
  37.7 60.1 %collective-permute-start.51 = (bf16[256,2048]{1,0:T(8,128)(2,1)}, bf16[256,2048]{1,0:T(8,128)(2,1)}, u32[]{:S(2)}, u32[]{:S(2)}) collective-permute-start(bf16[256,2048]{1,0:T(8,128)(2,1)} %param.5), channel_id=1, source_target_pairs={{0,4},{2,6},{4,0},{6,2},{1,5},{3,7},{5,1},{7,3},{8,12},{10,14},{12... | collective-permute-start | bytes 3145736 | tf_op jit(solution)/shard_map/ppermute | solution.py:95
  40.8 25.6 %collective-permute-start.1 = (bf16[64,4096]{1,0:T(8,128)(2,1)S(1)}, bf16[64,4096]{1,0:T(8,128)(2,1)S(1)}, u32[]{:S(2)}, u32[]{:S(2)}) collective-permute-start(bf16[64,4096]{1,0:T(8,128)(2,1)S(1)} %get-tuple-element.80), channel_id=1, source_target_pairs={{0,8},{8,16},{16,24},{1,9},{9,17},{17,25},{2,10},{10,18},{18,26},{... | collective-permute-start | bytes 1572872 | tf_op jit(solution)/shard_map/ppermute | solution.py:31
  66.4 47.5 %collective-permute-start.60 = (bf16[256,2048]{1,0:T(8,128)(2,1)}, bf16[256,2048]{1,0:T(8,128)(2,1)}, u32[]{:S(2)}, u32[]{:S(2)}) collective-permute-start(bf16[256,2048]{1,0:T(8,128)(2,1)} %param.5), channel_id=1, source_target_pairs={{0,6},{2,4},{4,2},{6,0},{1,7},{3,5},{5,3},{7,1},{8,14},{10,12},{12... | collective-permute-start | bytes 3145736 | tf_op jit(solution)/shard_map/ppermute | solution.py:95
  71.4 56.0 %collective-permute-start.96 = (bf16[256,2048]{1,0:T(8,128)(2,1)}, bf16[256,2048]{1,0:T(8,128)(2,1)}, u32[]{:S(2)}, u32[]{:S(2)}) collective-permute-start(bf16[256,2048]{1,0:T(8,128)(2,1)} %param.5), channel_id=1, source_target_pairs={{0,1},{1,0},{2,3},{3,2},{4,5},{5,4},{6,7},{7,6},{8,9},{9,8},{10,11... | collective-permute-start | bytes 3145736 | tf_op jit(solution)/shard_map/ppermute | solution.py:98
  72.7 59.4 %collective-permute-start.5 = (bf16[64,4096]{1,0:T(8,128)(2,1)}, bf16[64,4096]{1,0:T(8,128)(2,1)S(1)}, u32[]{:S(2)}, u32[]{:S(2)}) collective-permute-start(bf16[64,4096]{1,0:T(8,128)(2,1)} %get-tuple-element.79), channel_id=1, source_target_pairs={{8,0},{16,8},{24,16},{9,1},{17,9},{25,17},{10,2},{18,10},{26,18},{... | collective-permute-start | bytes 1572872 | tf_op jit(solution)/shard_map/ppermute | solution.py:31
  80.9 51.7 %collective-permute-start.2 = (bf16[64,4096]{1,0:T(8,128)(2,1)}, bf16[64,4096]{1,0:T(8,128)(2,1)S(1)}, u32[]{:S(2)}, u32[]{:S(2)}) collective-permute-start(bf16[64,4096]{1,0:T(8,128)(2,1)} %get-tuple-element.78), channel_id=1, source_target_pairs={{0,8},{8,16},{16,24},{1,9},{9,17},{17,25},{2,10},{10,18},{18,26},{... | collective-permute-start | bytes 1572872 | tf_op jit(solution)/shard_map/ppermute | solution.py:31
  97.9 35.5 %collective-permute-start.14 = (bf16[64,4096]{1,0:T(8,128)(2,1)}, bf16[64,4096]{1,0:T(8,128)(2,1)}, u32[]{:S(2)}, u32[]{:S(2)}) collective-permute-start(bf16[64,4096]{1,0:T(8,128)(2,1)} %get-tuple-element.72), channel_id=1, source_target_pairs={{0,8},{8,16},{16,24},{1,9},{9,17},{17,25},{2,10},{10,18},{18,26},{... | collective-permute-start | bytes 1572872 | tf_op jit(solution)/shard_map/ppermute | solution.py:31
  113.9 24.2 %collective-permute-start.17 = (bf16[64,4096]{1,0:T(8,128)(2,1)}, bf16[64,4096]{1,0:T(8,128)(2,1)}, u32[]{:S(2)}, u32[]{:S(2)}) collective-permute-start(bf16[64,4096]{1,0:T(8,128)(2,1)} %get-tuple-element.73), channel_id=1, source_target_pairs={{8,0},{16,8},{24,16},{9,1},{17,9},{25,17},{10,2},{18,10},{26,18},{... | collective-permute-start | bytes 1572872 | tf_op jit(solution)/shard_map/ppermute | solution.py:31
  127.3 43.8 %collective-permute-start.97 = (bf16[256,2048]{1,0:T(8,128)(2,1)}, bf16[256,2048]{1,0:T(8,128)(2,1)S(1)}, u32[]{:S(2)}, u32[]{:S(2)}) collective-permute-start(bf16[256,2048]{1,0:T(8,128)(2,1)} %collective-permute-done.41), channel_id=1, source_target_pairs={{0,1},{1,0},{2,3},{3,2},{4,5},{5,4},{6,7},{7,6},{8,9},{9,8},{10,11... | collective-permute-start | bytes 3145736 | tf_op jit(solution)/shard_map/ppermute | solution.py:98
  132.0 43.8 %collective-permute-start.98 = (bf16[256,2048]{1,0:T(8,128)(2,1)}, bf16[256,2048]{1,0:T(8,128)(2,1)S(1)}, u32[]{:S(2)}, u32[]{:S(2)}) collective-permute-start(bf16[256,2048]{1,0:T(8,128)(2,1)} %collective-permute-done.51), channel_id=1, source_target_pairs={{0,1},{1,0},{2,3},{3,2},{4,5},{5,4},{6,7},{7,6},{8,9},{9,8},{10,11... | collective-permute-start | bytes 3145736 | tf_op jit(solution)/shard_map/ppermute | solution.py:98
  132.6 52.0 %collective-permute-start.99 = (bf16[256,2048]{1,0:T(8,128)(2,1)}, bf16[256,2048]{1,0:T(8,128)(2,1)S(1)}, u32[]{:S(2)}, u32[]{:S(2)}) collective-permute-start(bf16[256,2048]{1,0:T(8,128)(2,1)} %collective-permute-done.60), channel_id=1, source_target_pairs={{0,1},{1,0},{2,3},{3,2},{4,5},{5,4},{6,7},{7,6},{8,9},{9,8},{10,11... | collective-permute-start | bytes 3145736 | tf_op jit(solution)/shard_map/ppermute | solution.py:98
  165.1 34.7 %collective-permute-start.11 = (bf16[64,4096]{1,0:T(8,128)(2,1)S(1)}, bf16[64,4096]{1,0:T(8,128)(2,1)S(1)}, u32[]{:S(2)}, u32[]{:S(2)}) collective-permute-start(bf16[64,4096]{1,0:T(8,128)(2,1)S(1)} %get-tuple-element.76), channel_id=1, source_target_pairs={{0,8},{8,16},{16,24},{1,9},{9,17},{17,25},{2,10},{10,18},{18,26},{... | collective-permute-start | bytes 1572872 | tf_op jit(solution)/shard_map/ppermute | solution.py:31
  169.5 30.3 %collective-permute-start.9 = (bf16[64,4096]{1,0:T(8,128)(2,1)S(1)}, bf16[64,4096]{1,0:T(8,128)(2,1)S(1)}, u32[]{:S(2)}, u32[]{:S(2)}) collective-permute-start(bf16[64,4096]{1,0:T(8,128)(2,1)S(1)} %get-tuple-element.77), channel_id=1, source_target_pairs={{8,0},{16,8},{24,16},{9,1},{17,9},{25,17},{10,2},{18,10},{26,18},{... | collective-permute-start | bytes 1572872 | tf_op jit(solution)/shard_map/ppermute | solution.py:31
  171.1 23.7 %collective-permute-start.19 = (bf16[64,4096]{1,0:T(8,128)(2,1)S(1)}, bf16[64,4096]{1,0:T(8,128)(2,1)S(1)}, u32[]{:S(2)}, u32[]{:S(2)}) collective-permute-start(bf16[64,4096]{1,0:T(8,128)(2,1)S(1)} %get-tuple-element.69), channel_id=1, source_target_pairs={{8,0},{16,8},{24,16},{9,1},{17,9},{25,17},{10,2},{18,10},{26,18},{... | collective-permute-start | bytes 1572872 | tf_op jit(solution)/shard_map/ppermute | solution.py:31
  175.8 19.0 %collective-permute-start.16 = (bf16[64,4096]{1,0:T(8,128)(2,1)S(1)}, bf16[64,4096]{1,0:T(8,128)(2,1)S(1)}, u32[]{:S(2)}, u32[]{:S(2)}) collective-permute-start(bf16[64,4096]{1,0:T(8,128)(2,1)S(1)} %get-tuple-element.68), channel_id=1, source_target_pairs={{0,8},{8,16},{16,24},{1,9},{9,17},{17,25},{2,10},{10,18},{18,26},{... | collective-permute-start | bytes 1572872 | tf_op jit(solution)/shard_map/ppermute | solution.py:31
  200.1 26.3 %collective-permute-start.10 = (bf16[64,4096]{1,0:T(8,128)(2,1)S(1)}, bf16[64,4096]{1,0:T(8,128)(2,1)S(1)}, u32[]{:S(2)}, u32[]{:S(2)}) collective-permute-start(bf16[64,4096]{1,0:T(8,128)(2,1)S(1)} %get-tuple-element.75), channel_id=1, source_target_pairs={{8,0},{16,8},{24,16},{9,1},{17,9},{25,17},{10,2},{18,10},{26,18},{... | collective-permute-start | bytes 1572872 | tf_op jit(solution)/shard_map/ppermute | solution.py:31
  201.4 25.0 %collective-permute-start.12 = (bf16[64,4096]{1,0:T(8,128)(2,1)S(1)}, bf16[64,4096]{1,0:T(8,128)(2,1)S(1)}, u32[]{:S(2)}, u32[]{:S(2)}) collective-permute-start(bf16[64,4096]{1,0:T(8,128)(2,1)S(1)} %get-tuple-element.74), channel_id=1, source_target_pairs={{0,8},{8,16},{16,24},{1,9},{9,17},{17,25},{2,10},{10,18},{18,26},{... | collective-permute-start | bytes 1572872 | tf_op jit(solution)/shard_map/ppermute | solution.py:31
  215.5 18.8 %collective-permute-start.25 = (bf16[64,4096]{1,0:T(8,128)(2,1)S(1)}, bf16[64,4096]{1,0:T(8,128)(2,1)S(1)}, u32[]{:S(2)}, u32[]{:S(2)}) collective-permute-start(bf16[64,4096]{1,0:T(8,128)(2,1)S(1)} %get-tuple-element.66), channel_id=1, source_target_pairs={{0,8},{8,16},{16,24},{1,9},{9,17},{17,25},{2,10},{10,18},{18,26},{... | collective-permute-start | bytes 1572872 | tf_op jit(solution)/shard_map/ppermute | solution.py:31
  218.2 19.4 %collective-permute-start.23 = (bf16[64,4096]{1,0:T(8,128)(2,1)S(1)}, bf16[64,4096]{1,0:T(8,128)(2,1)S(1)}, u32[]{:S(2)}, u32[]{:S(2)}) collective-permute-start(bf16[64,4096]{1,0:T(8,128)(2,1)S(1)} %get-tuple-element.67), channel_id=1, source_target_pairs={{8,0},{16,8},{24,16},{9,1},{17,9},{25,17},{10,2},{18,10},{26,18},{... | collective-permute-start | bytes 1572872 | tf_op jit(solution)/shard_map/ppermute | solution.py:31
  226.8 21.2 %collective-permute-start.29 = (bf16[64,4096]{1,0:T(8,128)(2,1)S(1)}, bf16[64,4096]{1,0:T(8,128)(2,1)S(1)}, u32[]{:S(2)}, u32[]{:S(2)}) collective-permute-start(bf16[64,4096]{1,0:T(8,128)(2,1)S(1)} %get-tuple-element.57), channel_id=1, source_target_pairs={{8,0},{16,8},{24,16},{9,1},{17,9},{25,17},{10,2},{18,10},{26,18},{... | collective-permute-start | bytes 1572872 | tf_op jit(solution)/shard_map/ppermute | solution.py:31
  228.1 19.9 %collective-permute-start.28 = (bf16[64,4096]{1,0:T(8,128)(2,1)S(1)}, bf16[64,4096]{1,0:T(8,128)(2,1)S(1)}, u32[]{:S(2)}, u32[]{:S(2)}) collective-permute-start(bf16[64,4096]{1,0:T(8,128)(2,1)S(1)} %get-tuple-element.56), channel_id=1, source_target_pairs={{0,8},{8,16},{16,24},{1,9},{9,17},{17,25},{2,10},{10,18},{18,26},{... | collective-permute-start | bytes 1572872 | tf_op jit(solution)/shard_map/ppermute | solution.py:31
  234.3 50.7 %collective-permute-start.92 = (bf16[256,2048]{1,0:T(8,128)(2,1)S(1)}, bf16[256,2048]{1,0:T(8,128)(2,1)S(1)}, u32[]{:S(2)}, u32[]{:S(2)}) collective-permute-start(bf16[256,2048]{1,0:T(8,128)(2,1)S(1)} %get-tuple-element.26), channel_id=1, source_target_pairs={{0,1},{1,0},{2,3},{3,2},{4,5},{5,4},{6,7},{7,6},{8,9},{9,8},{10,11... | collective-permute-start | bytes 3145736 | tf_op jit(solution)/shard_map/ppermute | solution.py:98
  238.0 17.1 %collective-permute-start.26 = (bf16[64,4096]{1,0:T(8,128)(2,1)S(1)}, bf16[64,4096]{1,0:T(8,128)(2,1)S(1)}, u32[]{:S(2)}, u32[]{:S(2)}) collective-permute-start(bf16[64,4096]{1,0:T(8,128)(2,1)S(1)} %get-tuple-element.64), channel_id=1, source_target_pairs={{0,8},{8,16},{16,24},{1,9},{9,17},{17,25},{2,10},{10,18},{18,26},{... | collective-permute-start | bytes 1572872 | tf_op jit(solution)/shard_map/ppermute | solution.py:31
  240.7 18.5 %collective-permute-start.24 = (bf16[64,4096]{1,0:T(8,128)(2,1)S(1)}, bf16[64,4096]{1,0:T(8,128)(2,1)S(1)}, u32[]{:S(2)}, u32[]{:S(2)}) collective-permute-start(bf16[64,4096]{1,0:T(8,128)(2,1)S(1)} %get-tuple-element.65), channel_id=1, source_target_pairs={{8,0},{16,8},{24,16},{9,1},{17,9},{25,17},{10,2},{18,10},{26,18},{... | collective-permute-start | bytes 1572872 | tf_op jit(solution)/shard_map/ppermute | solution.py:31
  248.6 17.7 %collective-permute-start.30 = (bf16[64,4096]{1,0:T(8,128)(2,1)S(1)}, bf16[64,4096]{1,0:T(8,128)(2,1)S(1)}, u32[]{:S(2)}, u32[]{:S(2)}) collective-permute-start(bf16[64,4096]{1,0:T(8,128)(2,1)S(1)} %get-tuple-element.15), channel_id=1, source_target_pairs={{0,8},{8,16},{16,24},{1,9},{9,17},{17,25},{2,10},{10,18},{18,26},{... | collective-permute-start | bytes 1572872 | tf_op jit(solution)/shard_map/ppermute | solution.py:31
  252.2 18.3 %collective-permute-start.31 = (bf16[64,4096]{1,0:T(8,128)(2,1)S(1)}, bf16[64,4096]{1,0:T(8,128)(2,1)S(1)}, u32[]{:S(2)}, u32[]{:S(2)}) collective-permute-start(bf16[64,4096]{1,0:T(8,128)(2,1)S(1)} %get-tuple-element.15), channel_id=1, source_target_pairs={{8,0},{16,8},{24,16},{9,1},{17,9},{25,17},{10,2},{18,10},{26,18},{... | collective-permute-start | bytes 1572872 | tf_op jit(solution)/shard_map/ppermute | solution.py:31
  259.6 28.3 %collective-permute-start.38 = (bf16[64,4096]{1,0:T(8,128)(2,1)S(1)}, bf16[64,4096]{1,0:T(8,128)(2,1)S(1)}, u32[]{:S(2)}, u32[]{:S(2)}) collective-permute-start(bf16[64,4096]{1,0:T(8,128)(2,1)S(1)} %get-tuple-element.63), channel_id=1, source_target_pairs={{8,0},{16,8},{24,16},{9,1},{17,9},{25,17},{10,2},{18,10},{26,18},{... | collective-permute-start | bytes 1572872 | tf_op jit(solution)/shard_map/ppermute | solution.py:31
  260.9 27.0 %collective-permute-start.37 = (bf16[64,4096]{1,0:T(8,128)(2,1)S(1)}, bf16[64,4096]{1,0:T(8,128)(2,1)S(1)}, u32[]{:S(2)}, u32[]{:S(2)}) collective-permute-start(bf16[64,4096]{1,0:T(8,128)(2,1)S(1)} %get-tuple-element.62), channel_id=1, source_target_pairs={{0,8},{8,16},{16,24},{1,9},{9,17},{17,25},{2,10},{10,18},{18,26},{... | collective-permute-start | bytes 1572872 | tf_op jit(solution)/shard_map/ppermute | solution.py:31
  270.8 22.4 %collective-permute-start.34 = (bf16[64,4096]{1,0:T(8,128)(2,1)S(1)}, bf16[64,4096]{1,0:T(8,128)(2,1)S(1)}, u32[]{:S(2)}, u32[]{:S(2)}) collective-permute-start(bf16[64,4096]{1,0:T(8,128)(2,1)S(1)} %get-tuple-element.54), channel_id=1, source_target_pairs={{0,8},{8,16},{16,24},{1,9},{9,17},{17,25},{2,10},{10,18},{18,26},{... | collective-permute-start | bytes 1572872 | tf_op jit(solution)/shard_map/ppermute | solution.py:31
  274.0 20.5 %collective-permute-start.32 = (bf16[64,4096]{1,0:T(8,128)(2,1)S(1)}, bf16[64,4096]{1,0:T(8,128)(2,1)S(1)}, u32[]{:S(2)}, u32[]{:S(2)}) collective-permute-start(bf16[64,4096]{1,0:T(8,128)(2,1)S(1)} %get-tuple-element.55), channel_id=1, source_target_pairs={{8,0},{16,8},{24,16},{9,1},{17,9},{25,17},{10,2},{18,10},{26,18},{... | collective-permute-start | bytes 1572872 | tf_op jit(solution)/shard_map/ppermute | solution.py:31
  285.0 156.8 %collective-permute-start.27 = (bf16[256,2048]{1,0:T(8,128)(2,1)}, bf16[256,2048]{1,0:T(8,128)(2,1)}, u32[]{:S(2)}, u32[]{:S(2)}) collective-permute-start(bf16[256,2048]{1,0:T(8,128)(2,1)} %convolution_convert_fusion.14), channel_id=1, source_target_pairs={{0,2},{2,0},{4,6},{6,4},{1,3},{3,1},{5,7},{7,5},{8,10},{10,8},{12,... | collective-permute-start | bytes 3145736 | tf_op jit(solution)/shard_map/ppermute | solution.py:95
  287.8 44.3 %collective-permute-start.93 = (bf16[256,2048]{1,0:T(8,128)(2,1)S(1)}, bf16[256,2048]{1,0:T(8,128)(2,1)S(1)}, u32[]{:S(2)}, u32[]{:S(2)}) collective-permute-start(bf16[256,2048]{1,0:T(8,128)(2,1)S(1)} %get-tuple-element.24), channel_id=1, source_target_pairs={{0,1},{1,0},{2,3},{3,2},{4,5},{5,4},{6,7},{7,6},{8,9},{9,8},{10,11... | collective-permute-start | bytes 3145736 | tf_op jit(solution)/shard_map/ppermute | solution.py:98
  294.8 25.5 %collective-permute-start.33 = (bf16[64,4096]{1,0:T(8,128)(2,1)S(1)}, bf16[64,4096]{1,0:T(8,128)(2,1)S(1)}, u32[]{:S(2)}, u32[]{:S(2)}) collective-permute-start(bf16[64,4096]{1,0:T(8,128)(2,1)S(1)} %get-tuple-element.53), channel_id=1, source_target_pairs={{8,0},{16,8},{24,16},{9,1},{17,9},{25,17},{10,2},{18,10},{26,18},{... | collective-permute-start | bytes 1572872 | tf_op jit(solution)/shard_map/ppermute | solution.py:31
  310.1 25.6 %collective-permute-start.44 = (bf16[64,4096]{1,0:T(8,128)(2,1)S(1)}, bf16[64,4096]{1,0:T(8,128)(2,1)S(1)}, u32[]{:S(2)}, u32[]{:S(2)}) collective-permute-start(bf16[64,4096]{1,0:T(8,128)(2,1)S(1)} %get-tuple-element.60), channel_id=1, source_target_pairs={{0,8},{8,16},{16,24},{1,9},{9,17},{17,25},{2,10},{10,18},{18,26},{... | collective-permute-start | bytes 1572872 | tf_op jit(solution)/shard_map/ppermute | solution.py:31
  320.4 20.6 %collective-permute-start.42 = (bf16[64,4096]{1,0:T(8,128)(2,1)S(1)}, bf16[64,4096]{1,0:T(8,128)(2,1)S(1)}, u32[]{:S(2)}, u32[]{:S(2)}) collective-permute-start(bf16[64,4096]{1,0:T(8,128)(2,1)S(1)} %get-tuple-element.61), channel_id=1, source_target_pairs={{8,0},{16,8},{24,16},{9,1},{17,9},{25,17},{10,2},{18,10},{26,18},{... | collective-permute-start | bytes 1572872 | tf_op jit(solution)/shard_map/ppermute | solution.py:31
  331.3 114.4 %collective-permute-start.36 = (bf16[256,2048]{1,0:T(8,128)(2,1)}, bf16[256,2048]{1,0:T(8,128)(2,1)S(1)}, u32[]{:S(2)}, u32[]{:S(2)}) collective-permute-start(bf16[256,2048]{1,0:T(8,128)(2,1)} %convolution_convert_fusion.13), channel_id=1, source_target_pairs={{0,4},{2,6},{4,0},{6,2},{1,5},{3,7},{5,1},{7,3},{8,12},{10,14},{12... | collective-permute-start | bytes 3145736 | tf_op jit(solution)/shard_map/ppermute | solution.py:95
  341.0 45.8 %collective-permute-start.94 = (bf16[256,2048]{1,0:T(8,128)(2,1)S(1)}, bf16[256,2048]{1,0:T(8,128)(2,1)S(1)}, u32[]{:S(2)}, u32[]{:S(2)}) collective-permute-start(bf16[256,2048]{1,0:T(8,128)(2,1)S(1)} %get-tuple-element.22), channel_id=1, source_target_pairs={{0,1},{1,0},{2,3},{3,2},{4,5},{5,4},{6,7},{7,6},{8,9},{9,8},{10,11... | collective-permute-start | bytes 3145736 | tf_op jit(solution)/shard_map/ppermute | solution.py:98
  361.6 17.1 %collective-permute-start.49 = (bf16[64,4096]{1,0:T(8,128)(2,1)S(1)}, bf16[64,4096]{1,0:T(8,128)(2,1)S(1)}, u32[]{:S(2)}, u32[]{:S(2)}) collective-permute-start(bf16[64,4096]{1,0:T(8,128)(2,1)S(1)} %get-tuple-element.11), channel_id=1, source_target_pairs={{0,8},{8,16},{16,24},{1,9},{9,17},{17,25},{2,10},{10,18},{18,26},{... | collective-permute-start | bytes 1572872 | tf_op jit(solution)/shard_map/ppermute | solution.py:31
  378.7 68.4 %collective-permute-start.46 = (bf16[256,2048]{1,0:T(8,128)(2,1)}, bf16[256,2048]{1,0:T(8,128)(2,1)S(1)}, u32[]{:S(2)}, u32[]{:S(2)}) collective-permute-start(bf16[256,2048]{1,0:T(8,128)(2,1)} %convolution_convert_fusion.12), channel_id=1, source_target_pairs={{0,6},{2,4},{4,2},{6,0},{1,7},{3,5},{5,3},{7,1},{8,14},{10,12},{12... | collective-permute-start | bytes 3145736 | tf_op jit(solution)/shard_map/ppermute | solution.py:95
  435.5 227.5 %collective-permute-start.84 = (bf16[256,2048]{1,0:T(8,128)(2,1)}, bf16[256,2048]{1,0:T(8,128)(2,1)}, u32[]{:S(2)}, u32[]{:S(2)}) collective-permute-start(bf16[256,2048]{1,0:T(8,128)(2,1)} %param.4), channel_id=1, source_target_pairs={{0,1},{1,0},{2,3},{3,2},{4,5},{5,4},{6,7},{7,6},{8,9},{9,8},{10,11... | collective-permute-start | bytes 3145736 | tf_op jit(solution)/shard_map/ppermute | solution.py:98
  441.5 18.9 %collective-permute-start.95 = (bf16[256,2048]{1,0:T(8,128)(2,1)S(1)}, bf16[256,2048]{1,0:T(8,128)(2,1)S(1)}, u32[]{:S(2)}, u32[]{:S(2)}) collective-permute-start(bf16[256,2048]{1,0:T(8,128)(2,1)S(1)} %get-tuple-element.20), channel_id=1, source_target_pairs={{0,1},{1,0},{2,3},{3,2},{4,5},{5,4},{6,7},{7,6},{8,9},{9,8},{10,11... | collective-permute-start | bytes 3145736 | tf_op jit(solution)/shard_map/ppermute | solution.py:98
  441.8 24.8 %collective-permute-start.63 = (bf16[64,4096]{1,0:T(8,128)(2,1)S(1)}, bf16[64,4096]{1,0:T(8,128)(2,1)S(1)}, u32[]{:S(2)}, u32[]{:S(2)}) collective-permute-start(bf16[64,4096]{1,0:T(8,128)(2,1)S(1)} %get-tuple-element.42), channel_id=1, source_target_pairs={{0,8},{8,16},{16,24},{1,9},{9,17},{17,25},{2,10},{10,18},{18,26},{... | collective-permute-start | bytes 1572872 | tf_op jit(solution)/shard_map/ppermute | solution.py:31
  445.8 20.9 %collective-permute-start.61 = (bf16[64,4096]{1,0:T(8,128)(2,1)S(1)}, bf16[64,4096]{1,0:T(8,128)(2,1)S(1)}, u32[]{:S(2)}, u32[]{:S(2)}) collective-permute-start(bf16[64,4096]{1,0:T(8,128)(2,1)S(1)} %get-tuple-element.43), channel_id=1, source_target_pairs={{8,0},{16,8},{24,16},{9,1},{17,9},{25,17},{10,2},{18,10},{26,18},{... | collective-permute-start | bytes 1572872 | tf_op jit(solution)/shard_map/ppermute | solution.py:31
  447.1 25.9 %collective-permute-start.67 = (bf16[64,4096]{1,0:T(8,128)(2,1)S(1)}, bf16[64,4096]{1,0:T(8,128)(2,1)S(1)}, u32[]{:S(2)}, u32[]{:S(2)}) collective-permute-start(bf16[64,4096]{1,0:T(8,128)(2,1)S(1)} %get-tuple-element.37), channel_id=1, source_target_pairs={{8,0},{16,8},{24,16},{9,1},{17,9},{25,17},{10,2},{18,10},{26,18},{... | collective-permute-start | bytes 1572872 | tf_op jit(solution)/shard_map/ppermute | solution.py:31
  460.3 17.5 %collective-permute-start.66 = (bf16[64,4096]{1,0:T(8,128)(2,1)S(1)}, bf16[64,4096]{1,0:T(8,128)(2,1)S(1)}, u32[]{:S(2)}, u32[]{:S(2)}) collective-permute-start(bf16[64,4096]{1,0:T(8,128)(2,1)S(1)} %get-tuple-element.36), channel_id=1, source_target_pairs={{0,8},{8,16},{16,24},{1,9},{9,17},{17,25},{2,10},{10,18},{18,26},{... | collective-permute-start | bytes 1572872 | tf_op jit(solution)/shard_map/ppermute | solution.py:31
  467.0 22.1 %collective-permute-start.64 = (bf16[64,4096]{1,0:T(8,128)(2,1)S(1)}, bf16[64,4096]{1,0:T(8,128)(2,1)S(1)}, u32[]{:S(2)}, u32[]{:S(2)}) collective-permute-start(bf16[64,4096]{1,0:T(8,128)(2,1)S(1)} %get-tuple-element.40), channel_id=1, source_target_pairs={{0,8},{8,16},{16,24},{1,9},{9,17},{17,25},{2,10},{10,18},{18,26},{... | collective-permute-start | bytes 1572872 | tf_op jit(solution)/shard_map/ppermute | solution.py:31
  470.9 18.2 %collective-permute-start.62 = (bf16[64,4096]{1,0:T(8,128)(2,1)S(1)}, bf16[64,4096]{1,0:T(8,128)(2,1)S(1)}, u32[]{:S(2)}, u32[]{:S(2)}) collective-permute-start(bf16[64,4096]{1,0:T(8,128)(2,1)S(1)} %get-tuple-element.41), channel_id=1, source_target_pairs={{8,0},{16,8},{24,16},{9,1},{17,9},{25,17},{10,2},{18,10},{26,18},{... | collective-permute-start | bytes 1572872 | tf_op jit(solution)/shard_map/ppermute | solution.py:31
  481.1 34.2 %collective-permute-start.68 = (bf16[64,4096]{1,0:T(8,128)(2,1)}, bf16[64,4096]{1,0:T(8,128)(2,1)}, u32[]{:S(2)}, u32[]{:S(2)}) collective-permute-start(bf16[64,4096]{1,0:T(8,128)(2,1)} %get-tuple-element.7), channel_id=1, source_target_pairs={{0,8},{8,16},{16,24},{1,9},{9,17},{17,25},{2,10},{10,18},{18,26},{... | collective-permute-start | bytes 1572872 | tf_op jit(solution)/shard_map/ppermute | solution.py:31
  490.3 25.0 %collective-permute-start.76 = (bf16[64,4096]{1,0:T(8,128)(2,1)}, bf16[64,4096]{1,0:T(8,128)(2,1)}, u32[]{:S(2)}, u32[]{:S(2)}) collective-permute-start(bf16[64,4096]{1,0:T(8,128)(2,1)} %get-tuple-element.39), channel_id=1, source_target_pairs={{8,0},{16,8},{24,16},{9,1},{17,9},{25,17},{10,2},{18,10},{26,18},{... | collective-permute-start | bytes 1572872 | tf_op jit(solution)/shard_map/ppermute | solution.py:31
  491.6 32.2 %collective-permute-start.75 = (bf16[64,4096]{1,0:T(8,128)(2,1)}, bf16[64,4096]{1,0:T(8,128)(2,1)}, u32[]{:S(2)}, u32[]{:S(2)}) collective-permute-start(bf16[64,4096]{1,0:T(8,128)(2,1)} %get-tuple-element.38), channel_id=1, source_target_pairs={{0,8},{8,16},{16,24},{1,9},{9,17},{17,25},{2,10},{10,18},{18,26},{... | collective-permute-start | bytes 1572872 | tf_op jit(solution)/shard_map/ppermute | solution.py:31
  503.3 19.2 %collective-permute-start.70 = (bf16[64,4096]{1,0:T(8,128)(2,1)}, bf16[64,4096]{1,0:T(8,128)(2,1)}, u32[]{:S(2)}, u32[]{:S(2)}) collective-permute-start(bf16[64,4096]{1,0:T(8,128)(2,1)} %collective-permute-done.69), channel_id=1, source_target_pairs={{8,0},{16,8},{24,16},{9,1},{17,9},{25,17},{10,2},{18,10},{26,18},{... | collective-permute-start | bytes 1572872 | tf_op jit(solution)/shard_map/ppermute | solution.py:31
  515.3 131.0 %collective-permute-start.89 = (bf16[256,2048]{1,0:T(8,128)(2,1)}, bf16[256,2048]{1,0:T(8,128)(2,1)}, u32[]{:S(2)}, u32[]{:S(2)}) collective-permute-start(bf16[256,2048]{1,0:T(8,128)(2,1)} %collective-permute-done.22), channel_id=1, source_target_pairs={{0,1},{1,0},{2,3},{3,2},{4,5},{5,4},{6,7},{7,6},{8,9},{9,8},{10,11... | collective-permute-start | bytes 3145736 | tf_op jit(solution)/shard_map/ppermute | solution.py:98
  526.4 17.1 %collective-permute-start.77 = (bf16[64,4096]{1,0:T(8,128)(2,1)S(1)}, bf16[64,4096]{1,0:T(8,128)(2,1)S(1)}, u32[]{:S(2)}, u32[]{:S(2)}) collective-permute-start(bf16[64,4096]{1,0:T(8,128)(2,1)S(1)} %get-tuple-element.9), channel_id=1, source_target_pairs={{0,8},{8,16},{16,24},{1,9},{9,17},{17,25},{2,10},{10,18},{18,26},{... | collective-permute-start | bytes 1572872 | tf_op jit(solution)/shard_map/ppermute | solution.py:31
  536.0 18.3 %collective-permute-start.73 = (bf16[64,4096]{1,0:T(8,128)(2,1)S(1)}, bf16[64,4096]{1,0:T(8,128)(2,1)S(1)}, u32[]{:S(2)}, u32[]{:S(2)}) collective-permute-start(bf16[64,4096]{1,0:T(8,128)(2,1)S(1)} %collective-permute-done.72), channel_id=1, source_target_pairs={{0,8},{8,16},{16,24},{1,9},{9,17},{17,25},{2,10},{10,18},{18,26},{... | collective-permute-start | bytes 1572872 | tf_op jit(solution)/shard_map/ppermute | solution.py:31
  543.5 88.1 %collective-permute-start.65 = (bf16[256,2048]{1,0:T(8,128)(2,1)}, bf16[256,2048]{1,0:T(8,128)(2,1)}, u32[]{:S(2)}, u32[]{:S(2)}) collective-permute-start(bf16[256,2048]{1,0:T(8,128)(2,1)} %convolution_convert_fusion.10), channel_id=1, source_target_pairs={{0,2},{2,0},{4,6},{6,4},{1,3},{3,1},{5,7},{7,5},{8,10},{10,8},{12,... | collective-permute-start | bytes 3145736 | tf_op jit(solution)/shard_map/ppermute | solution.py:95
  554.4 21.4 %collective-permute-start.81 = (bf16[64,4096]{1,0:T(8,128)(2,1)S(1)}, bf16[64,4096]{1,0:T(8,128)(2,1)}, u32[]{:S(2)}, u32[]{:S(2)}) collective-permute-start(bf16[64,4096]{1,0:T(8,128)(2,1)S(1)} %collective-permute-done.77), channel_id=1, source_target_pairs={{0,8},{8,16},{16,24},{1,9},{9,17},{17,25},{2,10},{10,18},{18,26},{... | collective-permute-start | bytes 1572872 | tf_op jit(solution)/shard_map/ppermute | solution.py:31
  575.7 55.9 %collective-permute-start.74 = (bf16[256,2048]{1,0:T(8,128)(2,1)}, bf16[256,2048]{1,0:T(8,128)(2,1)}, u32[]{:S(2)}, u32[]{:S(2)}) collective-permute-start(bf16[256,2048]{1,0:T(8,128)(2,1)} %convolution_convert_fusion.9), channel_id=1, source_target_pairs={{0,4},{2,6},{4,0},{6,2},{1,5},{3,7},{5,1},{7,3},{8,12},{10,14},{12... | collective-permute-start | bytes 3145736 | tf_op jit(solution)/shard_map/ppermute | solution.py:95
  599.7 32.4 %collective-permute-start.83 = (bf16[256,2048]{1,0:T(8,128)(2,1)}, bf16[256,2048]{1,0:T(8,128)(2,1)S(1)}, u32[]{:S(2)}, u32[]{:S(2)}) collective-permute-start(bf16[256,2048]{1,0:T(8,128)(2,1)} %convolution_convert_fusion.8), channel_id=1, source_target_pairs={{0,6},{2,4},{4,2},{6,0},{1,7},{3,5},{5,3},{7,1},{8,14},{10,12},{12... | collective-permute-start | bytes 3145736 | tf_op jit(solution)/shard_map/ppermute | solution.py:95
  646.8 17.3 %collective-permute-start.87 = (bf16[256,2048]{1,0:T(8,128)(2,1)}, bf16[256,2048]{1,0:T(8,128)(2,1)S(1)}, u32[]{:S(2)}, u32[]{:S(2)}) collective-permute-start(bf16[256,2048]{1,0:T(8,128)(2,1)} %get-tuple-element.31), channel_id=1, source_target_pairs={{0,1},{1,0},{2,3},{3,2},{4,5},{5,4},{6,7},{7,6},{8,9},{9,8},{10,11... | collective-permute-start | bytes 3145736 | tf_op jit(solution)/shard_map/ppermute | solution.py:98
  (62 other events, 848.3 us)

commit v2 on v0

v2 whole, which is shorter than its diff:
```python
import functools
import math

import jax
import jax.numpy as jnp
from jax import lax
from jax.experimental import pallas as pl
from jax.experimental.pallas import tpu as pltpu
from jax.sharding import PartitionSpec as P

F32, BF16 = jnp.float32, jnp.bfloat16
MESH = pl.DeviceIdType.MESH


def gelu_parts(pre):
    cdf = 0.5 * (1.0 + jax.scipy.special.erf(pre * (1.0 / math.sqrt(2.0))))
    activated = pre * cdf
    slope = cdf + pre * jnp.exp(-0.5 * pre * pre) * (1.0 / math.sqrt(2.0 * math.pi))
    return (activated, slope)


def line_kernel(
    n, cols, tok_ref, cot_ref, win_ref, wout_ref, ptok_ref, pcot_ref, full_ref,
    parts, outgo, land, stage, slope, tok_buf, win_buf, wout_buf,
    send_sem, recv_sem, gsend_sem, grecv_sem, local_sem, load_sem,
):
    rows, hidden = tok_ref.shape[0], win_ref.shape[1]
    shard, width = rows // n, hidden // n
    z, me = lax.axis_index("row"), lax.axis_index("col")
    strip = min(512, hidden)

    barrier = pltpu.get_barrier_semaphore()

    @pl.when(z > 0)
    def _():
        pl.semaphore_signal(barrier, inc=1, device_id={"row": z - 1}, device_id_type=MESH)

    @pl.when(z < n - 1)
    def _():
        pl.semaphore_signal(barrier, inc=1, device_id={"row": z + 1}, device_id_type=MESH)

    for k in range(1, cols):
        peer = lax.rem(me + k, cols)
        pl.semaphore_signal(barrier, inc=1, device_id={"col": peer}, device_id_type=MESH)

    @pl.when(jnp.logical_or(z == 0, z == n - 1))
    def _():
        pl.semaphore_wait(barrier, cols)

    @pl.when(jnp.logical_and(z > 0, z < n - 1))
    def _():
        pl.semaphore_wait(barrier, cols + 1)

    sources, panels = (tok_ref, cot_ref), (ptok_ref, pcot_ref)

    def gather(kind, k):
        return pltpu.make_async_remote_copy(
            src_ref=sources[kind], dst_ref=panels[kind].at[k],
            send_sem=gsend_sem.at[kind, k], recv_sem=grecv_sem.at[kind, k],
            device_id={"col": lax.rem(me + cols - k, cols)}, device_id_type=MESH,
        )

    for kind in range(2):
        for k in range(1, cols):
            gather(kind, k).start()
    own_copies = [
        pltpu.make_async_copy(sources[kind], panels[kind].at[0], local_sem.at[kind])
        for kind in range(2)
    ]
    for copy in own_copies:
        copy.start()
    for copy in own_copies:
        copy.wait()

    def weights_copy(kind, part):
        if kind == 0:
            src = win_ref.at[:, pl.ds(part * width, width)]
            return pltpu.make_async_copy(src, win_buf, load_sem.at[0])
        src = wout_ref.at[pl.ds(part * width, width), :]
        return pltpu.make_async_copy(src, wout_buf, load_sem.at[0])

    def tokens_copy(kind, k):
        return pltpu.make_async_copy(panels[kind].at[k], tok_buf, load_sem.at[1])

    def load(kind, k, part):
        weights_copy(kind, part).start()
        if part == 0:
            for slot in range(1, cols):
                @pl.when(k == slot)
                def _():
                    gather(kind, slot).wait_recv()
            tokens_copy(kind, k).start()

    def multiply(kind, k, part, half, chain):
        weights_copy(kind, part).wait()
        if part == 0:
            tokens_copy(kind, k).wait()
        step = min(width, 256)

        @pl.loop(0, width // step)
        def _(i):
            at = pl.multiple_of(i * step, step)
            if kind == 0:
                out = jnp.dot(tok_buf[...], win_buf[:, pl.ds(at, step)], preferred_element_type=F32)
            else:
                out = lax.dot_general(
                    tok_buf[...], wout_buf[pl.ds(at, step), :], (((1,), (1,)), ((), ())),
                    preferred_element_type=F32,
                )
            to = pl.multiple_of(part * width + i * step, step)
            parts[half, chain, :, :, pl.ds(to, step)] = out.astype(BF16).reshape(n, shard, step)

    def place(d):
        return z if d == 0 else n - 1 - z

    def real(d, q):
        return q if d == 0 else n - 1 - q

    def forms(s, d):
        p = place(d)
        if s == n:
            return p < n - 1, p >= 1
        return jnp.logical_and(p < n - 1, p < s), jnp.logical_and(p >= 1, p - 1 < s)

    def passes_on(s, d):
        p = place(d)
        return jnp.logical_and(p < n - 1, p >= s), jnp.logical_and(p >= 1, p - 1 >= s)

    def both(a, b):
        return jnp.logical_and(a, b)

    def copy_of(src, dst, s, c, d):
        return pltpu.make_async_remote_copy(
            src_ref=src, dst_ref=dst, send_sem=send_sem.at[s - 1, c, d],
            recv_sem=recv_sem.at[s - 1, c, d],
            device_id={"row": z + 1 if d == 0 else z - 1}, device_id_type=MESH,
        )

    def any_copy(s, c, d):
        return copy_of(stage.at[c], stage.at[c], s, c, d)

    def active(g, s, d, sending):
        which = 0 if sending else 1
        fresh = both(forms(s, d)[which], both(g >= 0, g < cols))
        if s > n - 2:
            return fresh
        old = both(passes_on(s, d)[which], both(g >= 1, g <= cols))
        return jnp.logical_or(fresh, old)

    def wait_recv(g, s, c):
        for d in range(2):
            @pl.when(active(g, s, d, False))
            def _():
                any_copy(s, c, d).wait_recv()

    def wait_send(g, s, c):
        for d in range(2):
            @pl.when(active(g, s, d, True))
            def _():
                any_copy(s, c, d).wait_send()

    def arrive(g, s, c):
        if s == 1:
            wait_recv(g - 1, n, c)
        else:
            wait_recv(g, s - 1, c)

    def pass_on(g, s, c):
        for d in range(2):
            @pl.when(both(passes_on(s, d)[0], g >= 1))
            def _():
                slot = full_ref.at[2 * (g - 1) + c, real(d, place(d) - s)]
                copy_of(slot, slot, s, c, d).start()

    def tick(g, s, c):
        half = lax.rem(g, 2)
        arrive(g, s, c)
        wait_send(g - 1, s, c)
        if s <= n - 2:
            pass_on(g, s, c)
        for d in range(2):
            @pl.when(forms(s, d)[0])
            def _():
                p = place(d)
                j = real(d, n - s + p)

                if s > 1:
                    @pl.when(p >= 1)
                    def _():
                        @pl.loop(0, hidden // strip)
                        def _(i):
                            at = pl.ds(pl.multiple_of(i * strip, strip), strip)
                            own = parts[half, c, j, :, at].astype(F32)
                            got = land[s - 2, c, d, :, at].astype(F32)
                            outgo[s - 1, c, d, :, at] = (own + got).astype(BF16)

                @pl.when(p == 0)
                def _():
                    outgo[s - 1, c, d] = parts[half, c, j]

                copy_of(outgo.at[s - 1, c, d], land.at[s - 1, c, d], s, c, d).start()

    def finish(g, c):
        half = lax.rem(g, 2)
        arrive(g, n, c)
        wait_send(g - 1, n, c)
        k = lax.rem(2 * g + c, cols)

        def total(at):
            own = parts[half, c, z, :, at].astype(F32)
            from_left = jnp.where(z > 0, land[n - 2, c, 0, :, at].astype(F32), 0.0)
            from_right = jnp.where(z < n - 1, land[n - 2, c, 1, :, at].astype(F32), 0.0)
            return own + from_left + from_right

        @pl.when(2 * g < cols)
        def _():
            @pl.loop(0, hidden // strip)
            def _(i):
                at = pl.ds(pl.multiple_of(i * strip, strip), strip)
                activated, steep = gelu_parts(total(at))
                slope[k, :, at] = steep
                stage[c, :, at] = activated.astype(BF16)

        @pl.when(2 * g >= cols)
        def _():
            @pl.loop(0, hidden // strip)
            def _(i):
                at = pl.ds(pl.multiple_of(i * strip, strip), strip)
                stage[c, :, at] = (total(at) * slope[k, :, at]).astype(BF16)

        slot = full_ref.at[2 * g + c, z]
        for d in range(2):
            @pl.when(forms(n, d)[0])
            def _():
                copy_of(stage.at[c], slot, n, c, d).start()
        keep = pltpu.make_async_copy(stage.at[c], slot, local_sem.at[0])
        keep.start()
        keep.wait()

    for c in range(2):
        for part in range(n):
            load(0, c, part)
            multiply(0, c, part, 0, c)
        if c == 0:
            tick(jnp.int32(0), 1, 0)

    @pl.loop(0, cols)
    def _(g):
        for s in range(1, n + 1):
            for c in range(2):
                piece = (s - 1) * 2 + c
                chain, part = piece // n, piece % n
                k = lax.rem(2 * (g + 1) + chain, cols)
                ahead_in = 2 * (g + 1) < cols
                ahead_out = both(2 * (g + 1) >= cols, g < cols - 1)
                for kind, ahead in enumerate((ahead_in, ahead_out)):
                    @pl.when(ahead)
                    def _():
                        load(kind, k, part)
                if s == n:
                    finish(g, c)
                elif s == 1 and c == 0:
                    @pl.when(g > 0)
                    def _():
                        tick(g, s, c)
                else:
                    tick(g, s, c)
                for kind, ahead in enumerate((ahead_in, ahead_out)):
                    @pl.when(ahead)
                    def _():
                        multiply(kind, k, part, lax.rem(g + 1, 2), chain)

    last = jnp.int32(cols)
    for s in range(1, n - 1):
        for c in range(2):
            arrive(last, s, c)
            wait_send(last - 1, s, c)
            pass_on(last, s, c)
    for c in range(2):
        if n > 2:
            wait_recv(last, n - 2, c)
        else:
            wait_recv(last - 1, n, c)
        for s in range(1, n - 1):
            wait_send(last, s, c)
        for s in (n - 1, n):
            wait_send(last - 1, s, c)
    for kind in range(2):
        for k in range(1, cols):
            gather(kind, k).wait_send()


def line_call(n, cols, tokens, out_grad, weight_in, weight_out):
    rows, depth = tokens.shape
    hidden = weight_in.shape[1]
    shard, width = rows // n, hidden // n
    return pl.pallas_call(
        functools.partial(line_kernel, n, cols),
        out_shape=[
            jax.ShapeDtypeStruct((cols, rows, depth), BF16),
            jax.ShapeDtypeStruct((cols, rows, depth), BF16),
            jax.ShapeDtypeStruct((2 * cols, n, shard, hidden), BF16),
        ],
        in_specs=[pl.BlockSpec(memory_space=pl.ANY)] * 4,
        out_specs=[pl.BlockSpec(memory_space=pl.ANY)] * 3,
        scratch_shapes=[
            pltpu.VMEM((2, 2, n, shard, hidden), BF16),
            pltpu.VMEM((n - 1, 2, 2, shard, hidden), BF16),
            pltpu.VMEM((n - 1, 2, 2, shard, hidden), BF16),
            pltpu.VMEM((2, shard, hidden), BF16),
            pltpu.VMEM((cols, shard, hidden), F32),
            pltpu.VMEM((rows, depth), BF16),
            pltpu.VMEM((depth, width), BF16),
            pltpu.VMEM((width, depth), BF16),
            pltpu.SemaphoreType.DMA((n, 2, 2)),
            pltpu.SemaphoreType.DMA((n, 2, 2)),
            pltpu.SemaphoreType.DMA((2, cols)),
            pltpu.SemaphoreType.DMA((2, cols)),
            pltpu.SemaphoreType.DMA((2,)),
            pltpu.SemaphoreType.DMA((2,)),
        ],
        compiler_params=pltpu.CompilerParams(
            collective_id=0, has_side_effects=True, vmem_limit_bytes=56 * 2**20
        ),
    )(tokens, out_grad, weight_in, weight_out)


def shards(tokens, out_grad, weight_in, weight_out):
    cols, n = lax.axis_size("col"), lax.axis_size("row")
    factor = 1.0 / math.sqrt(tokens.shape[0] * cols * lax.axis_size("dp"))
    hidden = weight_in.shape[1]
    half = hidden // 2
    core = lax.axis_index("dp")
    tok, cot, full = line_call(n, cols, tokens, out_grad, weight_in, weight_out)
    full = full.reshape(2, -1, hidden)
    tok, cot = tok.reshape(-1, tok.shape[-1]), cot.reshape(-1, cot.shape[-1])
    act, dpre = full[0], full[1]

    def home(part):
        part = part.astype(BF16).reshape(cols, -1, part.shape[-1])
        total = part[0].astype(F32)
        for k in range(1, cols):
            ring = [(i, (i + k) % cols) for i in range(cols)]
            total = total + lax.ppermute(part[k], "col", ring).astype(F32)
        return total.astype(BF16)

    def other(x):
        return lax.ppermute(x, "dp", [(0, 1), (1, 0)])

    def units(x):
        mine = lax.dynamic_slice_in_dim(x, core * half, half, 1)
        theirs = lax.dynamic_slice_in_dim(x, (1 - core) * half, half, 1)
        return jnp.concatenate([mine, other(theirs)], axis=0)

    def across(left, right):
        return lax.dot_general(left, right, (((0,), (0,)), ((), ())), preferred_element_type=F32)

    mixed = home(jnp.dot(act, weight_out, preferred_element_type=F32))
    token_grad = home(
        lax.dot_general(dpre, weight_in, (((1,), (1,)), ((), ())), preferred_element_type=F32)
    )
    grad_out = across(units(act), jnp.concatenate([cot, other(cot)], axis=0)) * factor
    grad_in = across(jnp.concatenate([tok, other(tok)], axis=0), units(dpre)) * factor
    return (mixed, token_grad, grad_in, grad_out)


def solution(mesh):
    placed = (P(("col", "dp"), "row"), P(("col", "dp"), "row"), P("row", "col"), P("col", "row"))
    return jax.shard_map(
        shards,
        mesh=mesh,
        in_specs=placed,
        out_specs=(
            P(("col", "dp"), "row"),
            P(("col", "dp"), "row"),
            P("row", ("col", "dp")),
            P(("col", "dp"), "row"),
        ),
        check_vma=False,
    )
```

time: 906 us -> 693 us (0.76)
  waiting for transfers between devices: 673 us -> 66.5 us
  Pallas kernels: 0 us -> 490 us
  matrix products: 147 us -> 86.9 us
  other arithmetic: 28.9 us -> 6.73 us
  between operations: 14.6 us -> 0.74 us
    pallas_call x0 -> x1, Pallas kernels: none -> 490 us  [line_call(): pl.pallas_call(functools.partial(line_kernel, n, cols), out_shape=[jax.Sh...]
    all_gather x4 -> x0, waiting for transfers between devices: 363 us -> none  [the longest x1 150 us: shards(): lax.all_gather((back * slope).astype(jnp.bfloat16), 'row', axis=0, tiled=...]
    reduce_scatter x6 -> x0, waiting for transfers between devices: 308 us -> none  [the longest x1 148 us: shards(): lax.psum_scatter(jnp.dot(panel, weight_in, preferred_element_type=jnp.flo...]
    ppermute x0 -> x10, waiting for transfers between devices: none -> 66.5 us  [the longest x6 66.5 us: home(): total = total + lax.ppermute(part[k], 'col', ring).astype(F32)]
    dot_general x5 -> x3, matrix products: 121 us -> 63.9 us  [the longest x2 46.1 us: across(): lax.dot_general(left, right, (((0,), (0,)), ((), ())), preferred_element_...]
    unnamed x2 -> x16, local copies, waits for them, and re-layouts: 35.5 us -> 8.48 us
    mul x2 -> x0, other arithmetic: 23.9 us -> none  [the longest x1 12.3 us: shards(): lax.psum_scatter(in_local.astype(jnp.bfloat16), 'dp', scatter_dimension=1...]
    slice x0 -> x3, local copies, waits for them, and re-layouts: none -> 12.9 us  [the longest x1 9.36 us: shards(): act, dpre = (full[0], full[1])]
  transfers between devices with their start and end apart: 10 -> 10, of which waited for: 7 -> 4; matrix products, arithmetic and copies ran while one was open for 23% -> 10% of each run, Pallas kernels for 0% -> 0%
where the time goes in v2:
time: 693 us
  Pallas kernels  490 us (71%)
  matrix products  86.9 us (13%)
  waiting for transfers between devices  66.5 us (10%)
  local copies, waits for them, and re-layouts  34 us (5%)
  starting transfers between devices  7.46 us (1%)
    pallas_call x1, Pallas kernels, line_call(): pl.pallas_call(functools.partial(line_kernel, n, cols), out_shape=[jax.Sh...  490 us
    ppermute x6, waiting for transfers between devices, home(): total = total + lax.ppermute(part[k], 'col', ring).astype(F32)  66.5 us
    dot_general x2, matrix products, across(): lax.dot_general(left, right, (((0,), (0,)), ((), ())), preferred_element_...  46.1 us
    dot_general x1, matrix products, shards(): lax.dot_general(dpre, weight_in, (((1,), (1,)), ((), ())), preferred_elem...  23 us
    dot_general x1, matrix products, shards(): mixed = home(jnp.dot(act, weight_out, preferred_element_type=F32))  17.8 us
  transfers between devices with their start and end apart: 10, of which 4 were waited for; matrix products, arithmetic and copies ran while one was open for 10% of the time, Pallas kernels for 0%

profile of v2, /device:TPU:0, one launch (start us, length us, event | category | flops | bytes accessed | tf_op | source)
XLA Modules:
  0.0 692.8 jit_solution(4877618918581300168)
XLA Ops:
  0.6 490.4 %shard_map.75 = (bf16[4,256,2048]{2,1,0:T(8,128)(2,1)}, bf16[4,256,2048]{2,1,0:T(8,128)(2,1)}, bf16[8,4,64,4096]{3,2,1,0:T(8,128)(2,1)}) custom-call(bf16[256,2048]{1,0:T(8,128)(2,1)} %tok_ref.1, bf16[256,2048]{1,0:T(8,128)(2,1)} %cot_ref.1, bf16[2048,4096]{1,0:T(8,128)(2,1)} %win_ref.1, bf16[4096,2048]{1,0:T(8,128)(2,1)} %wout_ref.1), custom_call_target="tpu_custom_call" | custom-call | tf_op jit(solution)/shard_map/pallas_call | solution.py:297
  491.1 0.0 copy-start.1
  491.1 9.4 %fusion.14 = (bf16[4,4,64,4096]{3,2,1,0:T(8,128)(2,1)}, bf16[4,4,64,4096]{3,2,1,0:T(8,128)(2,1)S(1)}) fusion(bf16[8,4,64,4096]{3,2,1,0:T(8,128)(2,1)} %get-tuple-element.7), kind=kLoop, calls=%fused_computation.24 | loop fusion | bytes 33554432 | tf_op jit(solution)/shard_map/slice | solution.py:337
  500.5 0.0 copy-start
  500.5 7.3 %copy-done.1 = bf16[4096,2048]{1,0:T(8,128)(2,1)S(1)} copy-done((bf16[4096,2048]{1,0:T(8,128)(2,1)S(1)}, bf16[4096,2048]{1,0:T(8,128)(2,1)}, u32[]{:S(2)}) %copy-start.1) | copy-done | bytes 16777240
  507.8 17.8 %convolution_convert_fusion.1 = bf16[1024,2048]{1,0:T(8,128)(2,1)S(1)} fusion(bf16[1024,4096]{1,0:T(8,128)(2,1)S(1)} %bitcast.8, bf16[4096,2048]{1,0:T(8,128)(2,1)S(1)} %copy-done.1), kind=kOutput, calls=%fused_computation.15 | convolution fusion | flops 17181966336 | bytes 29360128 | tf_op jit(solution)/shard_map/dot_general | solution.py:358
  525.6 0.0 copy-done
  525.6 0.0 copy-start.2
  525.6 1.8 fusion.16
  527.4 1.1 copy-done.2
  528.5 0.6 collective-permute-start
  529.1 2.3 collective-permute-start.2
  531.4 0.7 collective-permute-start.1
  532.1 0.0 slice-start
  532.1 8.5 %constant_dynamic-slice_fusion.3 = (bf16[1024,2048]{1,0:T(8,128)(2,1)}, bf16[1024,2048]{1,0:T(8,128)(2,1)}) fusion(bf16[1024,4096]{1,0:T(8,128)(2,1)} %bitcast.12, s32[]{:T(128)S(6)} %select_n.8, s32[]{:T(128)S(6)} %select_n.9), kind=kLoop, calls=%fused_computation.21 | loop fusion | bytes 16777224 | tf_op jit(solution)/shard_map/dynamic_slice | solution.py:351
  540.6 0.0 collective-permute-start.7
  540.6 0.0 slice-start.1
  540.6 0.5 collective-permute-start.6
  541.1 23.0 %convolution_convert_fusion = bf16[1024,2048]{1,0:T(8,128)(2,1)S(1)} fusion(bf16[1024,4096]{1,0:T(8,128)(2,1)} %bitcast.13, bf16[2048,4096]{1,0:T(8,128)(2,1)} %win_ref.1), kind=kOutput, calls=%fused_computation.14 | convolution fusion | flops 17181966336 | bytes 29360128 | tf_op jit(solution)/shard_map/dot_general | solution.py:360
  564.1 1.7 fusion.15
  565.9 0.0 collective-permute-done
  565.9 0.6 collective-permute-start.3
  566.5 11.1 %collective-permute-done.2 = bf16[256,2048]{1,0:T(8,128)(2,1)} collective-permute-done((bf16[256,2048]{1,0:T(8,128)(2,1)}, bf16[256,2048]{1,0:T(8,128)(2,1)}, u32[]{:S(2)}, u32[]{:S(2)}) %collective-permute-start.2) | collective-permute-done | bytes 1048608 | tf_op jit(solution)/shard_map/ppermute | solution.py:344
  577.5 1.4 collective-permute-start.5
  579.0 0.0 slice-done
  579.0 0.0 slice-done.1
  579.0 4.2 constant_dynamic-slice_fusion.1
  583.2 0.0 copy-start.3
  583.2 0.0 collective-permute-done.1
  583.2 0.0 collective-permute-start.8
  583.2 17.6 %collective-permute-done.3 = bf16[256,2048]{1,0:T(8,128)(2,1)} collective-permute-done((bf16[256,2048]{1,0:T(8,128)(2,1)}, bf16[256,2048]{1,0:T(8,128)(2,1)}, u32[]{:S(2)}, u32[]{:S(2)}) %collective-permute-start.3) | collective-permute-done | bytes 1048608 | tf_op jit(solution)/shard_map/ppermute | solution.py:344
  600.8 0.0 collective-permute-start.9
  600.8 19.5 %collective-permute-done.5 = bf16[256,2048]{1,0:T(8,128)(2,1)} collective-permute-done((bf16[256,2048]{1,0:T(8,128)(2,1)}, bf16[256,2048]{1,0:T(8,128)(2,1)}, u32[]{:S(2)}, u32[]{:S(2)}) %collective-permute-start.5) | collective-permute-done | bytes 1048608 | tf_op jit(solution)/shard_map/ppermute | solution.py:344
  620.3 1.4 collective-permute-start.4
  621.6 3.5 add_convert_fusion.1
  625.2 18.3 %collective-permute-done.4 = bf16[256,2048]{1,0:T(8,128)(2,1)S(1)} collective-permute-done((bf16[256,2048]{1,0:T(8,128)(2,1)}, bf16[256,2048]{1,0:T(8,128)(2,1)S(1)}, u32[]{:S(2)}, u32[]{:S(2)}) %collective-permute-start.4) | collective-permute-done | bytes 1048608 | tf_op jit(solution)/shard_map/ppermute | solution.py:344
  643.5 3.2 add_convert_fusion
  646.7 0.0 collective-permute-done.7
  646.7 0.0 collective-permute-done.6
  646.7 0.0 copy-done.3
  646.7 0.0 copy-start.4
  646.7 0.0 copy-start.5
  646.7 23.6 %convolution_multiply_fusion.1 = f32[2048,2048]{1,0:T(8,128)} fusion(bf16[1024,2048]{1,0:T(8,128)(2,1)} %collective-permute-done.6, bf16[1024,2048]{1,0:T(8,128)(2,1)} %bitcast.2, bf16[1024,2048]{1,0:T(8,128)(2,1)} %collective-permute-done.7, bf16[1024,2048]{1,0:T(8,128)(2,1)S(1)} %copy-done.3), kind=kOutput, calls=%fused_computation.1 | convolution fusion | flops 17217617920 | bytes 33554432 | tf_op jit(solution)/shard_map/dot_general | solution.py:356
  670.3 0.0 collective-permute-done.8
  670.3 0.0 collective-permute-done.9
  670.3 0.0 copy-done.4
  670.3 0.0 copy-done.5
  670.4 22.4 %convolution_multiply_fusion = f32[2048,2048]{1,0:T(8,128)} fusion(bf16[1024,2048]{1,0:T(8,128)(2,1)S(1)} %collective-permute-done.8, bf16[1024,2048]{1,0:T(8,128)(2,1)S(1)} %copy-done.4, bf16[1024,2048]{1,0:T(8,128)(2,1)} %collective-permute-done.9, bf16[1024,2048]{1,0:T(8,128)(2,1)S(1)} %bitcast.15), kind=kOutput, calls=%fused_computation | convolution fusion | flops 17217617920 | bytes 33554432 | tf_op jit(solution)/shard_map/dot_general | solution.py:356
  (1 shorter events, 0.0 us)
Async XLA Ops:
  491.1 16.7 %copy-start.1 = (bf16[4096,2048]{1,0:T(8,128)(2,1)S(1)}, bf16[4096,2048]{1,0:T(8,128)(2,1)}, u32[]{:S(2)}) copy-start(bf16[4096,2048]{1,0:T(8,128)(2,1)} %wout_ref.1) | copy-start | bytes 50331652
  500.5 25.1 %copy-start = (bf16[4,4,64,4096]{3,2,1,0:T(8,128)(2,1)}, bf16[4,4,64,4096]{3,2,1,0:T(8,128)(2,1)S(1)}, u32[]{:S(2)}) copy-start(bf16[4,4,64,4096]{3,2,1,0:T(8,128)(2,1)S(1)} %get-tuple-element.11) | copy-start | bytes 25165828
  525.6 2.9 copy-start.2
  528.5 37.4 %collective-permute-start = (bf16[256,2048]{1,0:T(8,128)(2,1)}, bf16[256,2048]{1,0:T(8,128)(2,1)S(1)}, u32[]{:S(2)}, u32[]{:S(2)}) collective-permute-start(bf16[256,2048]{1,0:T(8,128)(2,1)} %get-tuple-element.19), channel_id=1, source_target_pairs={{0,2},{2,4},{4,6},{6,0},{1,3},{3,5},{5,7},{7,1},{8,10},{10,12},{12... | collective-permute-start | bytes 3145736 | tf_op jit(solution)/shard_map/ppermute | solution.py:344
  529.1 48.4 %collective-permute-start.2 = (bf16[256,2048]{1,0:T(8,128)(2,1)}, bf16[256,2048]{1,0:T(8,128)(2,1)}, u32[]{:S(2)}, u32[]{:S(2)}) collective-permute-start(bf16[256,2048]{1,0:T(8,128)(2,1)} %get-tuple-element.20), channel_id=1, source_target_pairs={{0,6},{2,0},{4,2},{6,4},{1,7},{3,1},{5,3},{7,5},{8,14},{10,8},{12,... | collective-permute-start | bytes 3145736 | tf_op jit(solution)/shard_map/ppermute | solution.py:344
  531.4 51.7 %collective-permute-start.1 = (bf16[256,2048]{1,0:T(8,128)(2,1)}, bf16[256,2048]{1,0:T(8,128)(2,1)}, u32[]{:S(2)}, u32[]{:S(2)}) collective-permute-start(bf16[256,2048]{1,0:T(8,128)(2,1)} %get-tuple-element.21), channel_id=1, source_target_pairs={{0,4},{2,6},{4,0},{6,2},{1,5},{3,7},{5,1},{7,3},{8,12},{10,14},{12... | collective-permute-start | bytes 3145736 | tf_op jit(solution)/shard_map/ppermute | solution.py:344
  532.1 46.9 %slice-start = ((s8[8388608]{0:T(1024)(128)(4,1)}), s8[4194304]{0:T(1024)(128)(4,1)S(1)}, s32[]{:S(2)}) async-start(s8[8388608]{0:T(1024)(128)(4,1)} %bitcast.9), calls=%async_computation | async-start | bytes 8388608
  540.6 106.1 %collective-permute-start.7 = (bf16[1024,2048]{1,0:T(8,128)(2,1)}, bf16[1024,2048]{1,0:T(8,128)(2,1)}, u32[]{:S(2)}, u32[]{:S(2)}) collective-permute-start(bf16[1024,2048]{1,0:T(8,128)(2,1)} %get-tuple-element.15), channel_id=1, source_target_pairs={{0,1},{1,0},{2,3},{3,2},{4,5},{5,4},{6,7},{7,6},{8,9},{9,8},{10,11... | collective-permute-start | bytes 12582920 | tf_op jit(solution)/shard_map/ppermute | solution.py:348
  540.6 38.4 %slice-start.1 = ((s8[8388608]{0:T(1024)(128)(4,1)}), s8[4194304]{0:T(1024)(128)(4,1)S(1)}, s32[]{:S(2)}) async-start(s8[8388608]{0:T(1024)(128)(4,1)} %bitcast.9), calls=%async_computation.1 | async-start | bytes 8388608
  540.6 106.1 %collective-permute-start.6 = (bf16[1024,2048]{1,0:T(8,128)(2,1)}, bf16[1024,2048]{1,0:T(8,128)(2,1)}, u32[]{:S(2)}, u32[]{:S(2)}) collective-permute-start(bf16[1024,2048]{1,0:T(8,128)(2,1)} %bitcast.2), channel_id=1, source_target_pairs={{0,1},{1,0},{2,3},{3,2},{4,5},{5,4},{6,7},{7,6},{8,9},{9,8},{10,11... | collective-permute-start | bytes 12582920 | tf_op jit(solution)/shard_map/ppermute | solution.py:348
  565.9 34.9 %collective-permute-start.3 = (bf16[256,2048]{1,0:T(8,128)(2,1)}, bf16[256,2048]{1,0:T(8,128)(2,1)}, u32[]{:S(2)}, u32[]{:S(2)}) collective-permute-start(bf16[256,2048]{1,0:T(8,128)(2,1)} %get-tuple-element.16), channel_id=1, source_target_pairs={{0,2},{2,4},{4,6},{6,0},{1,3},{3,5},{5,7},{7,1},{8,10},{10,12},{12... | collective-permute-start | bytes 3145736 | tf_op jit(solution)/shard_map/ppermute | solution.py:344
  577.5 42.7 %collective-permute-start.5 = (bf16[256,2048]{1,0:T(8,128)(2,1)}, bf16[256,2048]{1,0:T(8,128)(2,1)}, u32[]{:S(2)}, u32[]{:S(2)}) collective-permute-start(bf16[256,2048]{1,0:T(8,128)(2,1)} %get-tuple-element.17), channel_id=1, source_target_pairs={{0,6},{2,0},{4,2},{6,4},{1,7},{3,1},{5,3},{7,5},{8,14},{10,8},{12,... | collective-permute-start | bytes 3145736 | tf_op jit(solution)/shard_map/ppermute | solution.py:344
  583.2 63.5 %copy-start.3 = (bf16[1024,2048]{1,0:T(8,128)(2,1)S(1)}, bf16[1024,2048]{1,0:T(8,128)(2,1)}, u32[]{:S(2)}) copy-start(bf16[1024,2048]{1,0:T(8,128)(2,1)} %get-tuple-element.14) | copy-start | bytes 12582916
  583.2 87.2 %collective-permute-start.8 = (bf16[1024,2048]{1,0:T(8,128)(2,1)}, bf16[1024,2048]{1,0:T(8,128)(2,1)S(1)}, u32[]{:S(2)}, u32[]{:S(2)}) collective-permute-start(bf16[1024,2048]{1,0:T(8,128)(2,1)} %get-tuple-element.13), channel_id=1, source_target_pairs={{0,1},{1,0},{2,3},{3,2},{4,5},{5,4},{6,7},{7,6},{8,9},{9,8},{10,11... | collective-permute-start | bytes 12582920 | tf_op jit(solution)/shard_map/ppermute | solution.py:348
  600.8 69.5 %collective-permute-start.9 = (bf16[1024,2048]{1,0:T(8,128)(2,1)}, bf16[1024,2048]{1,0:T(8,128)(2,1)}, u32[]{:S(2)}, u32[]{:S(2)}) collective-permute-start(bf16[1024,2048]{1,0:T(8,128)(2,1)} %bitcast.14), channel_id=1, source_target_pairs={{0,1},{1,0},{2,3},{3,2},{4,5},{5,4},{6,7},{7,6},{8,9},{9,8},{10,11... | collective-permute-start | bytes 12582920 | tf_op jit(solution)/shard_map/ppermute | solution.py:348
  620.3 23.2 %collective-permute-start.4 = (bf16[256,2048]{1,0:T(8,128)(2,1)}, bf16[256,2048]{1,0:T(8,128)(2,1)S(1)}, u32[]{:S(2)}, u32[]{:S(2)}) collective-permute-start(bf16[256,2048]{1,0:T(8,128)(2,1)} %get-tuple-element.18), channel_id=1, source_target_pairs={{0,4},{2,6},{4,0},{6,2},{1,5},{3,7},{5,1},{7,3},{8,12},{10,14},{12... | collective-permute-start | bytes 3145736 | tf_op jit(solution)/shard_map/ppermute | solution.py:344
  646.7 23.7 %copy-start.4 = (bf16[1024,2048]{1,0:T(8,128)(2,1)S(1)}, bf16[1024,2048]{1,0:T(8,128)(2,1)}, u32[]{:S(2)}) copy-start(bf16[1024,2048]{1,0:T(8,128)(2,1)} %get-tuple-element.12) | copy-start | bytes 12582916
  646.7 23.7 %copy-start.5 = (bf16[4,256,2048]{2,1,0:T(8,128)(2,1)S(1)}, bf16[4,256,2048]{2,1,0:T(8,128)(2,1)}, u32[]{:S(2)}) copy-start(bf16[4,256,2048]{2,1,0:T(8,128)(2,1)} %get-tuple-element.9) | copy-start | bytes 12582916

commit v3 on v2

--- a/solution.py
+++ b/solution.py
@@ -20,14 +20,16 @@
 
 
 def line_kernel(
-    n, cols, tok_ref, cot_ref, win_ref, wout_ref, ptok_ref, pcot_ref, full_ref,
-    parts, outgo, land, stage, slope, tok_buf, win_buf, wout_buf,
+    n, cols, tok_ref, cot_ref, win_ref, wout_ref, ptok_ref, pcot_ref,
+    act_ref, dpre_ref, uact_ref, udpre_ref, parts, outgo, land, stage, slope, tok_buf, win_buf, wout_buf,
     send_sem, recv_sem, gsend_sem, grecv_sem, local_sem, load_sem,
+    psend_sem, precv_sem, usend_sem, urecv_sem, ulocal_sem,
 ):
     rows, hidden = tok_ref.shape[0], win_ref.shape[1]
     shard, width = rows // n, hidden // n
     z, me = lax.axis_index("row"), lax.axis_index("col")
     strip = min(512, hidden)
+    core, units = lax.axis_index("dp"), hidden // 2
 
     barrier = pltpu.get_barrier_semaphore()
 
@@ -39,23 +41,55 @@
     def _():
         pl.semaphore_signal(barrier, inc=1, device_id={"row": z + 1}, device_id_type=MESH)
 
+    pl.semaphore_signal(barrier, inc=1, device_id={"dp": 1 - core}, device_id_type=MESH)
     for k in range(1, cols):
         peer = lax.rem(me + k, cols)
         pl.semaphore_signal(barrier, inc=1, device_id={"col": peer}, device_id_type=MESH)
 
     @pl.when(jnp.logical_or(z == 0, z == n - 1))
     def _():
-        pl.semaphore_wait(barrier, cols)
+        pl.semaphore_wait(barrier, cols + 1)
 
     @pl.when(jnp.logical_and(z > 0, z < n - 1))
     def _():
-        pl.semaphore_wait(barrier, cols + 1)
+        pl.semaphore_wait(barrier, cols + 2)
 
     sources, panels = (tok_ref, cot_ref), (ptok_ref, pcot_ref)
+
+    fulls, halves = (act_ref, dpre_ref), (uact_ref, udpre_ref)
+
+    def partner(kind, k):
+        return pltpu.make_async_remote_copy(
+            src_ref=panels[kind].at[0, k], dst_ref=panels[kind].at[1, k],
+            send_sem=psend_sem.at[kind, k], recv_sem=precv_sem.at[kind, k],
+            device_id={"dp": 1 - core}, device_id_type=MESH,
+        )
+
+    def unit_send(kind, k):
+        theirs = pl.ds(pl.multiple_of((1 - core) * units, units), units)
+        return pltpu.make_async_remote_copy(
+            src_ref=fulls[kind].at[k, :, :, theirs], dst_ref=halves[kind].at[1, k],
+            send_sem=usend_sem.at[kind, k], recv_sem=urecv_sem.at[kind, k],
+            device_id={"dp": 1 - core}, device_id_type=MESH,
+        )
+
+    def unit_keep(kind, k):
+        mine = pl.ds(pl.multiple_of(core * units, units), units)
+        return pltpu.make_async_copy(
+            fulls[kind].at[k, :, :, mine], halves[kind].at[0, k], ulocal_sem.at[kind, k]
+        )
+
+    def share(g, c):
+        for kind in range(2):
+            @pl.when(jnp.logical_and(g >= 0, 2 * g >= cols if kind == 1 else 2 * g < cols))
+            def _():
+                k = lax.rem(2 * g + c, cols)
+                unit_send(kind, k).start()
+                unit_keep(kind, k).start()
 
     def gather(kind, k):
         return pltpu.make_async_remote_copy(
-            src_ref=sources[kind], dst_ref=panels[kind].at[k],
+            src_ref=sources[kind], dst_ref=panels[kind].at[0, k],
             send_sem=gsend_sem.at[kind, k], recv_sem=grecv_sem.at[kind, k],
             device_id={"col": lax.rem(me + cols - k, cols)}, device_id_type=MESH,
         )
@@ -64,13 +98,15 @@
         for k in range(1, cols):
             gather(kind, k).start()
     own_copies = [
-        pltpu.make_async_copy(sources[kind], panels[kind].at[0], local_sem.at[kind])
+        pltpu.make_async_copy(sources[kind], panels[kind].at[0, 0], local_sem.at[kind])
         for kind in range(2)
     ]
     for copy in own_copies:
         copy.start()
     for copy in own_copies:
         copy.wait()
+    for kind in range(2):
+        partner(kind, 0).start()
 
     def weights_copy(kind, part):
         if kind == 0:
@@ -80,7 +116,7 @@
         return pltpu.make_async_copy(src, wout_buf, load_sem.at[0])
 
     def tokens_copy(kind, k):
-        return pltpu.make_async_copy(panels[kind].at[k], tok_buf, load_sem.at[1])
+        return pltpu.make_async_copy(panels[kind].at[0, k], tok_buf, load_sem.at[1])
 
     def load(kind, k, part):
         weights_copy(kind, part).start()
@@ -89,6 +125,7 @@
                 @pl.when(k == slot)
                 def _():
                     gather(kind, slot).wait_recv()
+                    partner(kind, slot).start()
             tokens_copy(kind, k).start()
 
     def multiply(kind, k, part, half, chain):
@@ -167,10 +204,14 @@
 
     def pass_on(g, s, c):
         for d in range(2):
-            @pl.when(both(passes_on(s, d)[0], g >= 1))
-            def _():
-                slot = full_ref.at[2 * (g - 1) + c, real(d, place(d) - s)]
-                copy_of(slot, slot, s, c, d).start()
+            for kind in range(2):
+                early = 2 * (g - 1) >= cols if kind == 1 else 2 * (g - 1) < cols
+
+                @pl.when(both(both(passes_on(s, d)[0], g >= 1), early))
+                def _():
+                    k = lax.rem(2 * (g - 1) + c, cols)
+                    slot = fulls[kind].at[k, real(d, place(d) - s)]
+                    copy_of(slot, slot, s, c, d).start()
 
     def tick(g, s, c):
         half = lax.rem(g, 2)
@@ -178,6 +219,8 @@
         wait_send(g - 1, s, c)
         if s <= n - 2:
             pass_on(g, s, c)
+        if s == n - 1:
+            share(g - 1, c)
         for d in range(2):
             @pl.when(forms(s, d)[0])
             def _():
@@ -228,14 +271,17 @@
                 at = pl.ds(pl.multiple_of(i * strip, strip), strip)
                 stage[c, :, at] = (total(at) * slope[k, :, at]).astype(BF16)
 
-        slot = full_ref.at[2 * g + c, z]
-        for d in range(2):
-            @pl.when(forms(n, d)[0])
+        for kind in range(2):
+            @pl.when(2 * g >= cols if kind == 1 else 2 * g < cols)
             def _():
-                copy_of(stage.at[c], slot, n, c, d).start()
-        keep = pltpu.make_async_copy(stage.at[c], slot, local_sem.at[0])
-        keep.start()
-        keep.wait()
+                slot = fulls[kind].at[k, z]
+                for d in range(2):
+                    @pl.when(forms(n, d)[0])
+                    def _():
+                        copy_of(stage.at[c], slot, n, c, d).start()
+                keep = pltpu.make_async_copy(stage.at[c], slot, local_sem.at[0])
+                keep.start()
+                keep.wait()
 
     for c in range(2):
         for part in range(n):
@@ -281,6 +327,7 @@
             wait_recv(last, n - 2, c)
         else:
             wait_recv(last - 1, n, c)
+        share(last - 1, c)
         for s in range(1, n - 1):
             wait_send(last, s, c)
         for s in (n - 1, n):
@@ -288,6 +335,10 @@
     for kind in range(2):
         for k in range(1, cols):
             gather(kind, k).wait_send()
+        for k in range(cols):
+            partner(kind, k).wait()
+            unit_send(kind, k).wait()
+            unit_keep(kind, k).wait()
 
 
 def line_call(n, cols, tokens, out_grad, weight_in, weight_out):
@@ -297,12 +348,15 @@
     return pl.pallas_call(
         functools.partial(line_kernel, n, cols),
         out_shape=[
-            jax.ShapeDtypeStruct((cols, rows, depth), BF16),
-            jax.ShapeDtypeStruct((cols, rows, depth), BF16),
-            jax.ShapeDtypeStruct((2 * cols, n, shard, hidden), BF16),
+            jax.ShapeDtypeStruct((2, cols, rows, depth), BF16),
+            jax.ShapeDtypeStruct((2, cols, rows, depth), BF16),
+            jax.ShapeDtypeStruct((cols, n, shard, hidden), BF16),
+            jax.ShapeDtypeStruct((cols, n, shard, hidden), BF16),
+            jax.ShapeDtypeStruct((2, cols, n, shard, hidden // 2), BF16),
+            jax.ShapeDtypeStruct((2, cols, n, shard, hidden // 2), BF16),
         ],
         in_specs=[pl.BlockSpec(memory_space=pl.ANY)] * 4,
-        out_specs=[pl.BlockSpec(memory_space=pl.ANY)] * 3,
+        out_specs=[pl.BlockSpec(memory_space=pl.ANY)] * 6,
         scratch_shapes=[
             pltpu.VMEM((2, 2, n, shard, hidden), BF16),
             pltpu.VMEM((n - 1, 2, 2, shard, hidden), BF16),
@@ -318,6 +372,11 @@
             pltpu.SemaphoreType.DMA((2, cols)),
             pltpu.SemaphoreType.DMA((2,)),
             pltpu.SemaphoreType.DMA((2,)),
+            pltpu.SemaphoreType.DMA((2, cols)),
+            pltpu.SemaphoreType.DMA((2, cols)),
+            pltpu.SemaphoreType.DMA((2, cols)),
+            pltpu.SemaphoreType.DMA((2, cols)),
+            pltpu.SemaphoreType.DMA((2, cols)),
         ],
         compiler_params=pltpu.CompilerParams(
             collective_id=0, has_side_effects=True, vmem_limit_bytes=56 * 2**20
@@ -329,39 +388,41 @@
     cols, n = lax.axis_size("col"), lax.axis_size("row")
     factor = 1.0 / math.sqrt(tokens.shape[0] * cols * lax.axis_size("dp"))
     hidden = weight_in.shape[1]
-    half = hidden // 2
-    core = lax.axis_index("dp")
-    tok, cot, full = line_call(n, cols, tokens, out_grad, weight_in, weight_out)
-    full = full.reshape(2, -1, hidden)
+    tok, cot, act, dpre, act_units, dpre_units = line_call(
+        n, cols, tokens, out_grad, weight_in, weight_out
+    )
     tok, cot = tok.reshape(-1, tok.shape[-1]), cot.reshape(-1, cot.shape[-1])
-    act, dpre = full[0], full[1]
-
-    def home(part):
+    act, dpre = act.reshape(-1, hidden), dpre.reshape(-1, hidden)
+    act_units = act_units.reshape(-1, hidden // 2)
+    dpre_units = dpre_units.reshape(-1, hidden // 2)
+
+    def sent(part):
         part = part.astype(BF16).reshape(cols, -1, part.shape[-1])
-        total = part[0].astype(F32)
-        for k in range(1, cols):
-            ring = [(i, (i + k) % cols) for i in range(cols)]
-            total = total + lax.ppermute(part[k], "col", ring).astype(F32)
+        rings = [[(i, (i + k) % cols) for i in range(cols)] for k in range(1, cols)]
+        return [part[0]] + [lax.ppermute(part[k + 1], "col", rings[k]) for k in range(cols - 1)]
+
+    def summed(parts):
+        total = parts[0].astype(F32)
+        for part in parts[1:]:
+            total = total + part.astype(F32)
         return total.astype(BF16)
-
-    def other(x):
-        return lax.ppermute(x, "dp", [(0, 1), (1, 0)])
-
-    def units(x):
-        mine = lax.dynamic_slice_in_dim(x, core * half, half, 1)
-        theirs = lax.dynamic_slice_in_dim(x, (1 - core) * half, half, 1)
-        return jnp.concatenate([mine, other(theirs)], axis=0)
 
     def across(left, right):
         return lax.dot_general(left, right, (((0,), (0,)), ((), ())), preferred_element_type=F32)
 
-    mixed = home(jnp.dot(act, weight_out, preferred_element_type=F32))
-    token_grad = home(
+    mixed = sent(jnp.dot(act, weight_out, preferred_element_type=F32))
+    token_grad = sent(
         lax.dot_general(dpre, weight_in, (((1,), (1,)), ((), ())), preferred_element_type=F32)
     )
-    grad_out = across(units(act), jnp.concatenate([cot, other(cot)], axis=0)) * factor
-    grad_in = across(jnp.concatenate([tok, other(tok)], axis=0), units(dpre)) * factor
-    return (mixed, token_grad, grad_in, grad_out)
+    mixed[0], token_grad[0], act_units, tok = lax.optimization_barrier(
+        (mixed[0], token_grad[0], act_units, tok)
+    )
+    grad_out = across(act_units, cot) * factor
+    grad_in = across(tok, dpre_units) * factor
+    mixed, token_grad, grad_out, grad_in = lax.optimization_barrier(
+        (mixed, token_grad, grad_out, grad_in)
+    )
+    return (summed(mixed), summed(token_grad), grad_in, grad_out)
 
 
 def solution(mesh):

time: 693 us -> 688 us (level)
  Pallas kernels: 490 us -> 545 us
  local copies, waits for them, and re-layouts: 34 us -> 2.67 us
  waiting for transfers between devices: 66.5 us -> 39.1 us
    pallas_call x1, Pallas kernels: 490 us -> 545 us  [line_call(): pl.pallas_call(functools.partial(line_kernel, n, cols), out_shape=[jax.Sh...]
    ppermute x10 -> x6, waiting for transfers between devices: 66.5 us -> 39.1 us  [sent(): lax.ppermute(part[k + 1], 'col', rings[k])]
    dynamic_slice x2 -> x0, local copies, waits for them, and re-layouts: 12.7 us -> none  [units(): mine = lax.dynamic_slice_in_dim(x, core * half, half, 1)]
    slice x3 -> x1, local copies, waits for them, and re-layouts: 12.9 us -> 2.63 us  [sent(): part[k + 1]]
    unnamed x16, local copies, waits for them, and re-layouts: 8.48 us -> 0.04 us
  transfers between devices with their start and end apart: 10 -> 6, of which waited for: 4 -> 2; matrix products, arithmetic and copies ran while one was open for 10% -> 7% of each run, Pallas kernels for 0% -> 0%
where the time goes in v3:
time: 688 us
  Pallas kernels  545 us (79%)
  matrix products  89.4 us (13%)
  waiting for transfers between devices  39.1 us (6%)
  starting transfers between devices  7.04 us (1%)
    pallas_call x1, Pallas kernels, line_call(): pl.pallas_call(functools.partial(line_kernel, n, cols), out_shape=[jax.Sh...  545 us
    dot_general x2, matrix products, across(): lax.dot_general(left, right, (((0,), (0,)), ((), ())), preferred_element_...  45.1 us
    ppermute x6, waiting for transfers between devices, sent(): lax.ppermute(part[k + 1], 'col', rings[k])  39.1 us
    dot_general x1, matrix products, shards(): mixed = sent(jnp.dot(act, weight_out, preferred_element_type=F32))  22.8 us
    dot_general x1, matrix products, shards(): lax.dot_general(dpre, weight_in, (((1,), (1,)), ((), ())), preferred_elem...  21.5 us
  transfers between devices with their start and end apart: 6, of which 2 were waited for; matrix products, arithmetic and copies ran while one was open for 7% of the time, Pallas kernels for 0%

profile of v3, /device:TPU:0, one launch (start us, length us, event | category | flops | bytes accessed | tf_op | source)
XLA Modules:
  0.0 687.9 jit_solution(12381930011906786320)
XLA Ops:
  0.6 0.0 slice-start
  0.6 545.5 %shard_map.75 = (bf16[2,4,256,2048]{3,2,1,0:T(8,128)(2,1)}, bf16[2,4,256,2048]{3,2,1,0:T(8,128)(2,1)}, bf16[4,4,64,4096]{3,2,1,0:T(8,128)(2,1)}, bf16[4,4,64,409...) custom-call(bf16[256,2048]{1,0:T(8,128)(2,1)} %tok_ref.1, ...), custom_call_target="tpu_custom_call" | custom-call | tf_op jit(solution)/shard_map/pallas_call | solution.py:348
  546.1 0.0 slice-start.1
  546.1 0.0 slice-start.2
  546.2 0.0 slice-start.3
  546.2 22.8 %convolution_convert_fusion.1 = bf16[1024,2048]{1,0:T(8,128)(2,1)S(1)} fusion(bf16[1024,4096]{1,0:T(8,128)(2,1)} %bitcast.25, bf16[4096,2048]{1,0:T(8,128)(2,1)} %wout_ref.1), kind=kOutput, calls=%fused_computation.3 | convolution fusion | flops 17181966336 | bytes 29360128 | tf_op jit(solution)/shard_map/dot_general | solution.py:413
  569.0 0.0 slice-done
  569.0 0.0 slice-done.1
  569.0 0.0 slice-done.2
  569.0 0.0 slice-done.3
  569.1 21.5 %convolution_convert_fusion = bf16[1024,2048]{1,0:T(8,128)(2,1)} fusion(bf16[1024,4096]{1,0:T(8,128)(2,1)} %bitcast.24, bf16[2048,4096]{1,0:T(8,128)(2,1)S(1)} %bitcast.15), kind=kOutput, calls=%fused_computation.2 | convolution fusion | flops 17181966336 | bytes 29360128 | tf_op jit(solution)/shard_map/dot_general | solution.py:415
  590.5 0.0 slice-start.4
  590.5 0.0 slice-start.6
  590.5 2.6 fusion
  593.2 1.6 collective-permute-start.5
  594.8 0.5 collective-permute-start.4
  595.3 0.6 collective-permute-start.3
  595.9 2.4 collective-permute-start
  598.3 0.5 collective-permute-start.1
  598.8 0.0 slice-start.5
  598.8 0.0 slice-start.7
  598.8 24.5 %convolution_multiply_fusion.1 = f32[2048,2048]{1,0:T(8,128)} fusion(bf16[2048,2048]{1,0:T(8,128)(2,1)} %bitcast.23, bf16[2048,2048]{1,0:T(8,128)(2,1)} %bitcast.22), kind=kOutput, calls=%fused_computation.1 | convolution fusion | flops 17184063488 | bytes 33554432 | tf_op jit(solution)/shard_map/dot_general | solution.py:411
  623.3 0.0 collective-permute-done.5
  623.3 1.4 collective-permute-start.2
  624.7 0.0 slice-done.4
  624.7 0.0 slice-done.6
  624.7 0.0 slice-done.5
  624.7 0.0 slice-done.7
  624.7 20.6 %convolution_multiply_fusion = f32[2048,2048]{1,0:T(8,128)} fusion(bf16[2048,2048]{1,0:T(8,128)(2,1)S(1)} %bitcast.18, bf16[2048,2048]{1,0:T(8,128)(2,1)S(1)} %bitcast.21), kind=kOutput, calls=%fused_computation | convolution fusion | flops 17184063488 | bytes 33554432 | tf_op jit(solution)/shard_map/dot_general | solution.py:411
  645.4 20.5 %collective-permute-done.4 = bf16[256,2048]{1,0:T(8,128)(2,1)S(1)} collective-permute-done((bf16[256,2048]{1,0:T(8,128)(2,1)S(1)}, bf16[256,2048]{1,0:T(8,128)(2,1)S(1)}, u32[]{:S(2)}, u32[]{:S(2)}) %collective-permute-start.4) | collective-permute-done | bytes 1048608 | tf_op jit(solution)/shard_map/ppermute | solution.py:402
  665.8 0.0 collective-permute-done.3
  665.8 0.0 collective-permute-done
  665.8 18.7 %collective-permute-done.1 = bf16[256,2048]{1,0:T(8,128)(2,1)S(1)} collective-permute-done((bf16[256,2048]{1,0:T(8,128)(2,1)S(1)}, bf16[256,2048]{1,0:T(8,128)(2,1)S(1)}, u32[]{:S(2)}, u32[]{:S(2)}) %collective-permute-start.1) | collective-permute-done | bytes 1048608 | tf_op jit(solution)/shard_map/ppermute | solution.py:402
  684.5 0.0 collective-permute-done.2
  684.5 1.7 add_convert_fusion.1
  686.2 1.7 add_convert_fusion
  (3 shorter events, 0.0 us)
Async XLA Ops:
  0.6 568.4 %slice-start = ((s8[16777216]{0:T(1024)(128)(4,1)}), s8[4194304]{0:T(1024)(128)(4,1)S(1)}, s32[]{:S(2)}) async-start(s8[16777216]{0:T(1024)(128)(4,1)} %bitcast.14), calls=%async_computation | async-start | bytes 8388608
  546.1 22.9 %slice-start.1 = ((s8[16777216]{0:T(1024)(128)(4,1)}), s8[4194304]{0:T(1024)(128)(4,1)S(1)}, s32[]{:S(2)}) async-start(s8[16777216]{0:T(1024)(128)(4,1)} %bitcast.14), calls=%async_computation.1 | async-start | bytes 8388608
  546.1 22.9 %slice-start.2 = ((s8[16777216]{0:T(1024)(128)(4,1)}), s8[4194304]{0:T(1024)(128)(4,1)S(1)}, s32[]{:S(2)}) async-start(s8[16777216]{0:T(1024)(128)(4,1)} %bitcast.14), calls=%async_computation.2 | async-start | bytes 8388608
  546.2 22.9 %slice-start.3 = ((s8[16777216]{0:T(1024)(128)(4,1)}), s8[4194304]{0:T(1024)(128)(4,1)S(1)}, s32[]{:S(2)}) async-start(s8[16777216]{0:T(1024)(128)(4,1)} %bitcast.14), calls=%async_computation.3 | async-start | bytes 8388608
  590.5 34.2 %slice-start.4 = ((s8[8388608]{0:T(1024)(128)(4,1)}), s8[4194304]{0:T(1024)(128)(4,1)S(1)}, s32[]{:S(2)}) async-start(s8[8388608]{0:T(1024)(128)(4,1)} %bitcast.16), calls=%async_computation.4 | async-start | bytes 8388608
  590.5 34.2 %slice-start.6 = ((s8[8388608]{0:T(1024)(128)(4,1)}), s8[4194304]{0:T(1024)(128)(4,1)S(1)}, s32[]{:S(2)}) async-start(s8[8388608]{0:T(1024)(128)(4,1)} %bitcast.19), calls=%async_computation.6 | async-start | bytes 8388608
  593.2 30.1 %collective-permute-start.5 = (bf16[256,2048]{1,0:T(8,128)(2,1)S(1)}, bf16[256,2048]{1,0:T(8,128)(2,1)S(1)}, u32[]{:S(2)}, u32[]{:S(2)}) collective-permute-start(bf16[256,2048]{1,0:T(8,128)(2,1)S(1)} %get-tuple-element.44), channel_id=1, source_target_pairs={{0,6},{2,0},{4,2},{6,4},{1,7},{3,1},{5,3},{7,5},{8,14},{10,8},{12,... | collective-permute-start | bytes 3145736 | tf_op jit(solution)/shard_map/ppermute | solution.py:402
  594.8 71.0 %collective-permute-start.4 = (bf16[256,2048]{1,0:T(8,128)(2,1)S(1)}, bf16[256,2048]{1,0:T(8,128)(2,1)S(1)}, u32[]{:S(2)}, u32[]{:S(2)}) collective-permute-start(bf16[256,2048]{1,0:T(8,128)(2,1)S(1)} %get-tuple-element.45), channel_id=1, source_target_pairs={{0,4},{2,6},{4,0},{6,2},{1,5},{3,7},{5,1},{7,3},{8,12},{10,14},{12... | collective-permute-start | bytes 3145736 | tf_op jit(solution)/shard_map/ppermute | solution.py:402
  595.3 70.5 %collective-permute-start.3 = (bf16[256,2048]{1,0:T(8,128)(2,1)S(1)}, bf16[256,2048]{1,0:T(8,128)(2,1)S(1)}, u32[]{:S(2)}, u32[]{:S(2)}) collective-permute-start(bf16[256,2048]{1,0:T(8,128)(2,1)S(1)} %get-tuple-element.46), channel_id=1, source_target_pairs={{0,2},{2,4},{4,6},{6,0},{1,3},{3,5},{5,7},{7,1},{8,10},{10,12},{12... | collective-permute-start | bytes 3145736 | tf_op jit(solution)/shard_map/ppermute | solution.py:402
  595.9 69.9 %collective-permute-start = (bf16[256,2048]{1,0:T(8,128)(2,1)S(1)}, bf16[256,2048]{1,0:T(8,128)(2,1)S(1)}, u32[]{:S(2)}, u32[]{:S(2)}) collective-permute-start(bf16[256,2048]{1,0:T(8,128)(2,1)S(1)} %get-tuple-element.53), channel_id=1, source_target_pairs={{0,2},{2,4},{4,6},{6,0},{1,3},{3,5},{5,7},{7,1},{8,10},{10,12},{12... | collective-permute-start | bytes 3145736 | tf_op jit(solution)/shard_map/ppermute | solution.py:402
  598.3 86.2 %collective-permute-start.1 = (bf16[256,2048]{1,0:T(8,128)(2,1)S(1)}, bf16[256,2048]{1,0:T(8,128)(2,1)S(1)}, u32[]{:S(2)}, u32[]{:S(2)}) collective-permute-start(bf16[256,2048]{1,0:T(8,128)(2,1)S(1)} %get-tuple-element.54), channel_id=1, source_target_pairs={{0,4},{2,6},{4,0},{6,2},{1,5},{3,7},{5,1},{7,3},{8,12},{10,14},{12... | collective-permute-start | bytes 3145736 | tf_op jit(solution)/shard_map/ppermute | solution.py:402
  598.8 25.9 %slice-start.5 = ((s8[8388608]{0:T(1024)(128)(4,1)}), s8[4194304]{0:T(1024)(128)(4,1)S(1)}, s32[]{:S(2)}) async-start(s8[8388608]{0:T(1024)(128)(4,1)} %bitcast.16), calls=%async_computation.5 | async-start | bytes 8388608
  598.8 25.9 %slice-start.7 = ((s8[8388608]{0:T(1024)(128)(4,1)}), s8[4194304]{0:T(1024)(128)(4,1)S(1)}, s32[]{:S(2)}) async-start(s8[8388608]{0:T(1024)(128)(4,1)} %bitcast.19), calls=%async_computation.7 | async-start | bytes 8388608
  623.3 61.2 %collective-permute-start.2 = (bf16[256,2048]{1,0:T(8,128)(2,1)S(1)}, bf16[256,2048]{1,0:T(8,128)(2,1)S(1)}, u32[]{:S(2)}, u32[]{:S(2)}) collective-permute-start(bf16[256,2048]{1,0:T(8,128)(2,1)S(1)} %get-tuple-element.55), channel_id=1, source_target_pairs={{0,6},{2,0},{4,2},{6,4},{1,7},{3,1},{5,3},{7,5},{8,14},{10,8},{12,... | collective-permute-start | bytes 3145736 | tf_op jit(solution)/shard_map/ppermute | solution.py:402

commit v4 on v3

--- a/solution.py
+++ b/solution.py
@@ -28,7 +28,7 @@
     rows, hidden = tok_ref.shape[0], win_ref.shape[1]
     shard, width = rows // n, hidden // n
     z, me = lax.axis_index("row"), lax.axis_index("col")
-    strip = min(512, hidden)
+    strip = min(1024, hidden)
     core, units = lax.axis_index("dp"), hidden // 2
 
     barrier = pltpu.get_barrier_semaphore()
@@ -132,7 +132,7 @@
         weights_copy(kind, part).wait()
         if part == 0:
             tokens_copy(kind, k).wait()
-        step = min(width, 256)
+        step = min(width, 512)
 
         @pl.loop(0, width // step)
         def _(i):

time: 688 us -> 684 us (level)
  no operation moved by 1% of the time
where the time goes in v4:
time: 684 us
  Pallas kernels  542 us (79%)
  matrix products  89.4 us (13%)
  waiting for transfers between devices  39.1 us (6%)
  starting transfers between devices  7.04 us (1%)
    pallas_call x1, Pallas kernels, line_call(): pl.pallas_call(functools.partial(line_kernel, n, cols), out_shape=[jax.Sh...  542 us
    dot_general x2, matrix products, across(): lax.dot_general(left, right, (((0,), (0,)), ((), ())), preferred_element_...  45.1 us
    ppermute x6, waiting for transfers between devices, sent(): lax.ppermute(part[k + 1], 'col', rings[k])  39.1 us
    dot_general x1, matrix products, shards(): mixed = sent(jnp.dot(act, weight_out, preferred_element_type=F32))  23 us
    dot_general x1, matrix products, shards(): lax.dot_general(dpre, weight_in, (((1,), (1,)), ((), ())), preferred_elem...  21.3 us
  transfers between devices with their start and end apart: 6, of which 2 were waited for; matrix products, arithmetic and copies ran while one was open for 7% of the time, Pallas kernels for 0%

profile of v4, /device:TPU:0, one launch (start us, length us, event | category | flops | bytes accessed | tf_op | source)
XLA Modules:
  0.0 683.9 jit_solution(14833792854097029566)
XLA Ops:
  0.6 0.0 slice-start
  0.6 541.5 %shard_map.75 = (bf16[2,4,256,2048]{3,2,1,0:T(8,128)(2,1)}, bf16[2,4,256,2048]{3,2,1,0:T(8,128)(2,1)}, bf16[4,4,64,4096]{3,2,1,0:T(8,128)(2,1)}, bf16[4,4,64,409...) custom-call(bf16[256,2048]{1,0:T(8,128)(2,1)} %tok_ref.1, ...), custom_call_target="tpu_custom_call" | custom-call | tf_op jit(solution)/shard_map/pallas_call | solution.py:348
  542.2 0.0 slice-start.1
  542.2 0.0 slice-start.2
  542.2 0.0 slice-start.3
  542.2 23.0 %convolution_convert_fusion.1 = bf16[1024,2048]{1,0:T(8,128)(2,1)S(1)} fusion(bf16[1024,4096]{1,0:T(8,128)(2,1)} %bitcast.25, bf16[4096,2048]{1,0:T(8,128)(2,1)} %wout_ref.1), kind=kOutput, calls=%fused_computation.3 | convolution fusion | flops 17181966336 | bytes 29360128 | tf_op jit(solution)/shard_map/dot_general | solution.py:413
  565.2 0.0 slice-done
  565.2 0.0 slice-done.1
  565.3 0.0 slice-done.2
  565.3 0.0 slice-done.3
  565.3 21.3 %convolution_convert_fusion = bf16[1024,2048]{1,0:T(8,128)(2,1)} fusion(bf16[1024,4096]{1,0:T(8,128)(2,1)} %bitcast.24, bf16[2048,4096]{1,0:T(8,128)(2,1)S(1)} %bitcast.15), kind=kOutput, calls=%fused_computation.2 | convolution fusion | flops 17181966336 | bytes 29360128 | tf_op jit(solution)/shard_map/dot_general | solution.py:415
  586.6 0.0 slice-start.4
  586.6 0.0 slice-start.6
  586.6 2.6 fusion
  589.2 1.6 collective-permute-start.5
  590.8 0.5 collective-permute-start.4
  591.4 0.6 collective-permute-start.3
  591.9 2.4 collective-permute-start
  594.3 0.5 collective-permute-start.1
  594.8 0.0 slice-start.5
  594.8 0.0 slice-start.7
  594.9 24.5 %convolution_multiply_fusion.1 = f32[2048,2048]{1,0:T(8,128)} fusion(bf16[2048,2048]{1,0:T(8,128)(2,1)} %bitcast.23, bf16[2048,2048]{1,0:T(8,128)(2,1)} %bitcast.22), kind=kOutput, calls=%fused_computation.1 | convolution fusion | flops 17184063488 | bytes 33554432 | tf_op jit(solution)/shard_map/dot_general | solution.py:411
  619.3 0.0 collective-permute-done.5
  619.3 1.4 collective-permute-start.2
  620.8 0.0 slice-done.4
  620.8 0.0 slice-done.6
  620.8 0.0 slice-done.5
  620.8 0.0 slice-done.7
  620.8 20.6 %convolution_multiply_fusion = f32[2048,2048]{1,0:T(8,128)} fusion(bf16[2048,2048]{1,0:T(8,128)(2,1)S(1)} %bitcast.18, bf16[2048,2048]{1,0:T(8,128)(2,1)S(1)} %bitcast.21), kind=kOutput, calls=%fused_computation | convolution fusion | flops 17184063488 | bytes 33554432 | tf_op jit(solution)/shard_map/dot_general | solution.py:411
  641.4 20.5 %collective-permute-done.4 = bf16[256,2048]{1,0:T(8,128)(2,1)S(1)} collective-permute-done((bf16[256,2048]{1,0:T(8,128)(2,1)S(1)}, bf16[256,2048]{1,0:T(8,128)(2,1)S(1)}, u32[]{:S(2)}, u32[]{:S(2)}) %collective-permute-start.4) | collective-permute-done | bytes 1048608 | tf_op jit(solution)/shard_map/ppermute | solution.py:402
  661.9 0.0 collective-permute-done.3
  661.9 0.0 collective-permute-done
  661.9 18.6 %collective-permute-done.1 = bf16[256,2048]{1,0:T(8,128)(2,1)S(1)} collective-permute-done((bf16[256,2048]{1,0:T(8,128)(2,1)S(1)}, bf16[256,2048]{1,0:T(8,128)(2,1)S(1)}, u32[]{:S(2)}, u32[]{:S(2)}) %collective-permute-start.1) | collective-permute-done | bytes 1048608 | tf_op jit(solution)/shard_map/ppermute | solution.py:402
  680.5 0.0 collective-permute-done.2
  680.5 1.7 add_convert_fusion.1
  682.2 1.7 add_convert_fusion
  (3 shorter events, 0.0 us)
Async XLA Ops:
  0.6 564.6 %slice-start = ((s8[16777216]{0:T(1024)(128)(4,1)}), s8[4194304]{0:T(1024)(128)(4,1)S(1)}, s32[]{:S(2)}) async-start(s8[16777216]{0:T(1024)(128)(4,1)} %bitcast.14), calls=%async_computation | async-start | bytes 8388608
  542.2 23.1 %slice-start.1 = ((s8[16777216]{0:T(1024)(128)(4,1)}), s8[4194304]{0:T(1024)(128)(4,1)S(1)}, s32[]{:S(2)}) async-start(s8[16777216]{0:T(1024)(128)(4,1)} %bitcast.14), calls=%async_computation.1 | async-start | bytes 8388608
  542.2 23.1 %slice-start.2 = ((s8[16777216]{0:T(1024)(128)(4,1)}), s8[4194304]{0:T(1024)(128)(4,1)S(1)}, s32[]{:S(2)}) async-start(s8[16777216]{0:T(1024)(128)(4,1)} %bitcast.14), calls=%async_computation.2 | async-start | bytes 8388608
  542.2 23.1 %slice-start.3 = ((s8[16777216]{0:T(1024)(128)(4,1)}), s8[4194304]{0:T(1024)(128)(4,1)S(1)}, s32[]{:S(2)}) async-start(s8[16777216]{0:T(1024)(128)(4,1)} %bitcast.14), calls=%async_computation.3 | async-start | bytes 8388608
  586.6 34.2 %slice-start.4 = ((s8[8388608]{0:T(1024)(128)(4,1)}), s8[4194304]{0:T(1024)(128)(4,1)S(1)}, s32[]{:S(2)}) async-start(s8[8388608]{0:T(1024)(128)(4,1)} %bitcast.16), calls=%async_computation.4 | async-start | bytes 8388608
  586.6 34.2 %slice-start.6 = ((s8[8388608]{0:T(1024)(128)(4,1)}), s8[4194304]{0:T(1024)(128)(4,1)S(1)}, s32[]{:S(2)}) async-start(s8[8388608]{0:T(1024)(128)(4,1)} %bitcast.19), calls=%async_computation.6 | async-start | bytes 8388608
  589.2 30.1 %collective-permute-start.5 = (bf16[256,2048]{1,0:T(8,128)(2,1)S(1)}, bf16[256,2048]{1,0:T(8,128)(2,1)S(1)}, u32[]{:S(2)}, u32[]{:S(2)}) collective-permute-start(bf16[256,2048]{1,0:T(8,128)(2,1)S(1)} %get-tuple-element.44), channel_id=1, source_target_pairs={{0,6},{2,0},{4,2},{6,4},{1,7},{3,1},{5,3},{7,5},{8,14},{10,8},{12,... | collective-permute-start | bytes 3145736 | tf_op jit(solution)/shard_map/ppermute | solution.py:402
  590.8 71.0 %collective-permute-start.4 = (bf16[256,2048]{1,0:T(8,128)(2,1)S(1)}, bf16[256,2048]{1,0:T(8,128)(2,1)S(1)}, u32[]{:S(2)}, u32[]{:S(2)}) collective-permute-start(bf16[256,2048]{1,0:T(8,128)(2,1)S(1)} %get-tuple-element.45), channel_id=1, source_target_pairs={{0,4},{2,6},{4,0},{6,2},{1,5},{3,7},{5,1},{7,3},{8,12},{10,14},{12... | collective-permute-start | bytes 3145736 | tf_op jit(solution)/shard_map/ppermute | solution.py:402
  591.4 70.5 %collective-permute-start.3 = (bf16[256,2048]{1,0:T(8,128)(2,1)S(1)}, bf16[256,2048]{1,0:T(8,128)(2,1)S(1)}, u32[]{:S(2)}, u32[]{:S(2)}) collective-permute-start(bf16[256,2048]{1,0:T(8,128)(2,1)S(1)} %get-tuple-element.46), channel_id=1, source_target_pairs={{0,2},{2,4},{4,6},{6,0},{1,3},{3,5},{5,7},{7,1},{8,10},{10,12},{12... | collective-permute-start | bytes 3145736 | tf_op jit(solution)/shard_map/ppermute | solution.py:402
  591.9 70.0 %collective-permute-start = (bf16[256,2048]{1,0:T(8,128)(2,1)S(1)}, bf16[256,2048]{1,0:T(8,128)(2,1)S(1)}, u32[]{:S(2)}, u32[]{:S(2)}) collective-permute-start(bf16[256,2048]{1,0:T(8,128)(2,1)S(1)} %get-tuple-element.53), channel_id=1, source_target_pairs={{0,2},{2,4},{4,6},{6,0},{1,3},{3,5},{5,7},{7,1},{8,10},{10,12},{12... | collective-permute-start | bytes 3145736 | tf_op jit(solution)/shard_map/ppermute | solution.py:402
  594.3 86.2 %collective-permute-start.1 = (bf16[256,2048]{1,0:T(8,128)(2,1)S(1)}, bf16[256,2048]{1,0:T(8,128)(2,1)S(1)}, u32[]{:S(2)}, u32[]{:S(2)}) collective-permute-start(bf16[256,2048]{1,0:T(8,128)(2,1)S(1)} %get-tuple-element.54), channel_id=1, source_target_pairs={{0,4},{2,6},{4,0},{6,2},{1,5},{3,7},{5,1},{7,3},{8,12},{10,14},{12... | collective-permute-start | bytes 3145736 | tf_op jit(solution)/shard_map/ppermute | solution.py:402
  594.8 25.9 %slice-start.5 = ((s8[8388608]{0:T(1024)(128)(4,1)}), s8[4194304]{0:T(1024)(128)(4,1)S(1)}, s32[]{:S(2)}) async-start(s8[8388608]{0:T(1024)(128)(4,1)} %bitcast.16), calls=%async_computation.5 | async-start | bytes 8388608
  594.8 25.9 %slice-start.7 = ((s8[8388608]{0:T(1024)(128)(4,1)}), s8[4194304]{0:T(1024)(128)(4,1)S(1)}, s32[]{:S(2)}) async-start(s8[8388608]{0:T(1024)(128)(4,1)} %bitcast.19), calls=%async_computation.7 | async-start | bytes 8388608
  619.3 61.2 %collective-permute-start.2 = (bf16[256,2048]{1,0:T(8,128)(2,1)S(1)}, bf16[256,2048]{1,0:T(8,128)(2,1)S(1)}, u32[]{:S(2)}, u32[]{:S(2)}) collective-permute-start(bf16[256,2048]{1,0:T(8,128)(2,1)S(1)} %get-tuple-element.55), channel_id=1, source_target_pairs={{0,6},{2,0},{4,2},{6,4},{1,7},{3,1},{5,3},{7,5},{8,14},{10,8},{12,... | collective-permute-start | bytes 3145736 | tf_op jit(solution)/shard_map/ppermute | solution.py:402
